TPU v7x, 256 devices: a whole 4x4x8 slice. The times are simulated.
256 devices in a mesh: layer: 4 (over z_hi), tile: 64 (over y, z_lo, x, core).
Axes of the slice: x: 4, y: 4, z: 8 (z_hi: 4, z_lo: 2; z = z_hi * 2 + z_lo), core: 2. Of those that a mesh axis runs over, the one named last changes fastest.
Arguments:
- measured_slopes: float32 [6, 2, 768, 4096], P(None, None, 'tile'), may hold values from -18 to 18
- valid_mask: int32 [768, 4096], P('tile'), may hold values 0 or 1
- layer_offsets: int32 [6, 4, 2], replicated, may hold values from -8 to 8, as said below
- reg_weight: float32 [4], replicated, may hold values from 0.01 to 0.1
Outputs:
- layer_estimate: float32 [4, 768, 4096], P('layer', 'tile')
- residual: float32 [4, 768, 4096], P('layer', 'tile')
Inputs may be any that keep to these rules, and one draw needn't show every extreme that they name: `layer_offsets`: every entry lies between -8 and 8; some entry equals 8 and some equals -8.
All inputs are finite; a program needn't handle non-finite values. No bound on the sum of `valid_mask` on one device may be relied on, other than what follows from the above.
Results may differ from a plain program's by a relative error of at most 0.0001.
Values sent between devices are 32-bit elements; how exact they have to be, the bound alone decides.
A program may use at most 64 MiB of HBM per device.

v0:
```python
import jax
import jax.numpy as jnp
from jax import lax
from jax.sharding import PartitionSpec as P

LAY_DEV = 1
HALO = 8
ITERS = 2


def shifted(value, axis, steps):
    count = lax.axis_size(axis)
    first, last = (max(0, -steps), min(count, count - steps))
    return lax.ppermute(value, axis, [(source, source + steps) for source in range(first, last)])


def padded_2(cells, sides, width):
    for axis, dim in sides:
        count = lax.axis_size(axis)
        ends = count - 1
        head = lax.slice_in_dim(cells, 0, width, axis=dim)
        tail = lax.slice_in_dim(cells, cells.shape[dim] - width, cells.shape[dim], axis=dim)
        cells = jnp.concatenate(
            [
                lax.ppermute(tail, axis, [(i, (i + 1) % count) for i in range(ends)]),
                cells,
                lax.ppermute(head, axis, [((i + 1) % count, i) for i in range(ends)]),
            ],
            axis=dim,
        )
    return cells


def laplace_rows(field):
    padded = jnp.pad(field, ((0, 0), (0, 0), (1, 1)))
    center = field[:, 1:-1]
    return 4.0 * center - field[:, :-2] - field[:, 2:] - padded[:, 1:-1, :-2] - padded[:, 1:-1, 2:]


def per_device(measured_slopes, valid_mask, layer_offsets, reg_weight):
    dirs = measured_slopes.shape[0]
    rows = measured_slopes.shape[2]
    width = measured_slopes.shape[3]
    total_rows = rows * lax.axis_size("tile")
    first_row = lax.axis_index("tile") * rows
    layer_first = lax.axis_index("layer") * LAY_DEV
    maskf = valid_mask.astype(jnp.float32)
    own_offsets = lax.dynamic_slice_in_dim(layer_offsets, layer_first, LAY_DEV, 1)
    own_reg = lax.dynamic_slice_in_dim(reg_weight, layer_first, LAY_DEV, 0)

    def inside(start, count):
        index = first_row + start + jnp.arange(count)
        return ((index >= 0) & (index < total_rows)).astype(jnp.float32)[:, None]

    def left_of(field):
        return jnp.pad(field, ((0, 0), (0, 0), (1, 0)))[..., :width]

    def adjoint_field(slope_x, slope_y):
        above_x, above_y = shifted((slope_x[:, rows - 1 :], slope_y[:, rows - 1 :]), "tile", 1)
        upper_x = jnp.concatenate([above_x, slope_x[:, : rows - 1]], 1)
        summed_x = slope_x + upper_x
        summed_y = slope_y + left_of(slope_y)
        summed_above = above_y + left_of(above_y)
        upper_y = jnp.concatenate([summed_above, summed_y[:, : rows - 1]], 1)
        adjoint = 0.5 * (left_of(summed_x) - summed_x + upper_y - summed_y)
        return padded_2(adjoint, (("tile", 1),), HALO)

    def back_project(adjoint_ext):
        padded = jnp.pad(adjoint_ext, ((0, 0), (0, 0), (HALO, HALO)))

        def back_window(field, offset):
            return lax.dynamic_slice(field, (HALO - offset[0], HALO - offset[1]), (rows, width))

        result = [jnp.sum(jax.vmap(back_window)(padded, own_offsets[:, 0]), axis=0)]
        return jnp.stack(result)

    def squares(field):
        return lax.psum(jnp.sum(field * field), ("layer", "tile"))

    right_side = back_project(
        adjoint_field(maskf * measured_slopes[:, 0], maskf * measured_slopes[:, 1])
    )
    estimate = jnp.zeros_like(right_side)
    residual = right_side
    direction = right_side
    norm_now = squares(residual)
    for step in range(ITERS):
        apply_extended = padded_2(direction, (("tile", 1),), HALO + 1)
        extended = lax.all_gather(apply_extended, "layer", axis=0, tiled=True)
        project_padded = jnp.pad(extended, ((0, 0), (0, 0), (HALO, HALO)))
        total = jnp.zeros((dirs, rows + 1, width), jnp.float32)
        for project_member in range(extended.shape[0]):
            layer_pad = project_padded[project_member]

            def project_window(offset):
                return lax.dynamic_slice(
                    layer_pad, (HALO + 1 + offset[0], HALO + offset[1]), (rows + 1, width)
                )

            total = total + jax.vmap(project_window)(layer_offsets[:, project_member])
        apply_phase = total
        apply_phase = apply_phase * inside(0, rows + 1)[None]
        slopes_padded = jnp.pad(apply_phase, ((0, 0), (0, 0), (0, 1)))
        p00 = slopes_padded[:, :rows, :width]
        p01 = slopes_padded[:, :rows, 1:]
        p10 = slopes_padded[:, 1:, :width]
        p11 = slopes_padded[:, 1:, 1:]
        grad_x = 0.5 * (p01 - p00 + p11 - p10)
        grad_y = 0.5 * (p10 - p00 + p11 - p01)
        apply_slope_x = maskf * grad_x
        apply_slope_y = maskf * grad_y
        projected = back_project(adjoint_field(apply_slope_x, apply_slope_y))
        smoothed = (
            laplace_rows(apply_extended[:, HALO - 1 : HALO + rows + 3]) * inside(-1, rows + 2)[None]
        )
        image = projected + own_reg[:, None, None] * laplace_rows(smoothed)
        alpha = norm_now / lax.psum(jnp.sum(direction * image), ("layer", "tile"))
        estimate = estimate + alpha * direction
        residual = residual - alpha * image
        if step + 1 < ITERS:
            norm_next = squares(residual)
            direction = residual + norm_next / norm_now * direction
            norm_now = norm_next
    return (estimate, residual)


def solution(mesh):
    return jax.shard_map(
        per_device,
        mesh=mesh,
        in_specs=(P(None, None, "tile", None), P("tile", None), P(), P()),
        out_specs=(P("layer", "tile", None), P("layer", "tile", None)),
        check_vma=False,
    )
```

profile of v0, /device:TPU:1, one launch (start us, length us, event | category | flops | bytes accessed | tf_op | source)
XLA Modules:
  0.0 708.7 jit_solution(2479717395068278684)
XLA Ops:
  7.2 4.9 fusion.60
  13.1 4.5 collective-permute-start
  36.4 7.9 %collective-permute-done.3 = f32[6,8,4096]{2,1,0:T(8,128)S(1)} collective-permute-done((f32[6,8,4096]{2,1,0:T(8,128)}, f32[6,8,4096]{2,1,0:T(8,128)S(1)}, u32[]{:S(2)}, u32[]{:S(2)}) %collective-permute-start.3) | collective-permute-done | bytes 786464 | tf_op jit(solution)/shard_map/ppermute | solution.py:27
  49.6 22.3 %while.11 = (s32[]{:T(128)}, f32[6,28,4112]{2,1,0:T(8,128)}, s32[6,3]{0,1:T(4,128)S(1)}, f32[6,12,4096]{2,1,0:T(8,128)S(1)}, s32[]{:T(128)}) while((s32[]{:T(128)}, f32[6,28,4112]{2,1,0:T(8,128)}, s32[6,3]{0,1:T(4,128)S(1)}, f32[6,12,4096]{2,1,0:T(8,128)S(1)}, s32[]{:T(128)}) %tuple.198), condition=%wide.while_cond, body=%wide.while_body.sunk | while | flops 2 | bytes 458889 | solution.py:72
  74.0 4.4 collective-permute-start.4
  87.4 58.1 %all-gather.3.cloned.1.call-done = f32[4,30,4096]{2,1,0:T(8,128)} async-done(((f32[1,30,4096]{2,1,0:T(8,128)}), f32[4,30,4096]{2,1,0:T(8,128)}) %all-gather.3.cloned.1.call-update) | async-done | bytes 1966096 | tf_op jit(solution)/shard_map/all_gather | solution.py:89
  148.9 16.7 %while.15 = (s32[]{:T(128)}, f32[30,4112]{1,0:T(8,128)S(1)}, s32[6,2]{0,1:T(2,128)S(1)}, f32[6,13,4096]{2,1,0:T(8,128)}, s32[]{:T(128)}) while((s32[]{:T(128)}, f32[30,4112]{1,0:T(8,128)S(1)}, s32[6,2]{0,1:T(2,128)S(1)}, f32[6,13,4096]{2,1,0:T(8,128)}, s32[]{:T(128)}) %tuple.201), condition=%wide.while_cond.4, body=%wide.while_body.4.sunk | while | flops 2 | bytes 476269 | solution.py:96
  165.7 12.4 %while.14 = (s32[]{:T(128)}, f32[30,4112]{1,0:T(8,128)S(1)}, s32[6,2]{0,1:T(2,128)S(1)}, f32[6,13,4096]{2,1,0:T(8,128)S(1)}, s32[]{:T(128)}) while((s32[]{:T(128)}, f32[30,4112]{1,0:T(8,128)S(1)}, s32[6,2]{0,1:T(2,128)S(1)}, f32[6,13,4096]{2,1,0:T(8,128)S(1)}, s32[]{:T(128)}) %tuple.204), condition=%wide.while_cond.3, body=%wide.while_body.3.sunk | while | flops 2 | bytes 524405 | solution.py:96
  179.8 16.7 %while.12 = (s32[]{:T(128)}, f32[30,4112]{1,0:T(8,128)S(1)}, s32[6,2]{0,1:T(2,128)S(1)}, f32[6,13,4096]{2,1,0:T(8,128)}, s32[]{:T(128)}) while((s32[]{:T(128)}, f32[30,4112]{1,0:T(8,128)S(1)}, s32[6,2]{0,1:T(2,128)S(1)}, f32[6,13,4096]{2,1,0:T(8,128)}, s32[]{:T(128)}) %tuple.207), condition=%wide.while_cond.1, body=%wide.while_body.1.sunk | while | flops 2 | bytes 476269 | solution.py:96
  197.8 17.0 %while.13 = (s32[]{:T(128)}, f32[30,4112]{1,0:T(8,128)S(1)}, s32[6,2]{0,1:T(2,128)S(1)}, f32[6,13,4096]{2,1,0:T(8,128)}, s32[]{:T(128)}) while((s32[]{:T(128)}, f32[30,4112]{1,0:T(8,128)S(1)}, s32[6,2]{0,1:T(2,128)S(1)}, f32[6,13,4096]{2,1,0:T(8,128)}, s32[]{:T(128)}) %tuple.210), condition=%wide.while_cond.2, body=%wide.while_body.2.sunk | while | flops 2 | bytes 476269 | solution.py:96
  219.4 6.7 collective-permute-start.7
  238.4 7.5 %collective-permute-done.9 = f32[6,8,4096]{2,1,0:T(8,128)S(1)} collective-permute-done((f32[6,8,4096]{2,1,0:T(8,128)S(1)}, f32[6,8,4096]{2,1,0:T(8,128)S(1)}, u32[]{:S(2)}, u32[]{:S(2)}) %collective-permute-start.9) | collective-permute-done | bytes 786464 | tf_op jit(solution)/shard_map/ppermute | solution.py:27
  249.9 22.1 %while.16 = (s32[]{:T(128)}, f32[6,28,4112]{2,1,0:T(8,128)}, s32[6,3]{0,1:T(4,128)S(1)}, f32[6,12,4096]{2,1,0:T(8,128)S(1)}, s32[]{:T(128)}) while((s32[]{:T(128)}, f32[6,28,4112]{2,1,0:T(8,128)}, s32[6,3]{0,1:T(4,128)S(1)}, f32[6,12,4096]{2,1,0:T(8,128)S(1)}, s32[]{:T(128)}) %tuple.235), condition=%wide.while_cond.5, body=%wide.while_body.5.sunk | while | flops 2 | bytes 458889 | solution.py:72
  273.7 80.6 %all-reduce.20 = (f32[]{:T(128)}, f32[]{:T(128)}) all-reduce(f32[]{:T(128)} %multiply_reduce_fusion.3, f32[]{:T(128)} %get-tuple-element.184), channel_id=1, replica_groups=mesh['layer'=4,'tile'=64] {'layer','tile'}, use_global_device_ids=true, to_apply=%region_2.3 | all-reduce | flops 2 | bytes 16 | tf_op jit(solution)/shard_map/psum | solution.py:78
  356.1 73.3 %psum.30 = f32[]{:T(128)} all-reduce(f32[]{:T(128)} %multiply_reduce_fusion.1), channel_id=1, replica_groups=mesh['layer'=4,'tile'=64] {'layer','tile'}, use_global_device_ids=true, to_apply=%region_7.8 | all-reduce | flops 1 | bytes 8 | tf_op jit(solution)/shard_map/psum | solution.py:78
  442.2 48.0 %all-gather.5.cloned.1.call-done = f32[4,30,4096]{2,1,0:T(8,128)} async-done(((f32[1,30,4096]{2,1,0:T(8,128)}), f32[4,30,4096]{2,1,0:T(8,128)}) %all-gather.5.cloned.1.call-update) | async-done | bytes 1966096 | tf_op jit(solution)/shard_map/all_gather | solution.py:89
  493.6 16.7 %while.20 = (s32[]{:T(128)}, f32[30,4112]{1,0:T(8,128)S(1)}, s32[6,2]{0,1:T(2,128)S(1)}, f32[6,13,4096]{2,1,0:T(8,128)}, s32[]{:T(128)}) while((s32[]{:T(128)}, f32[30,4112]{1,0:T(8,128)S(1)}, s32[6,2]{0,1:T(2,128)S(1)}, f32[6,13,4096]{2,1,0:T(8,128)}, s32[]{:T(128)}) %tuple.240), condition=%wide.while_cond.9, body=%wide.while_body.9.sunk | while | flops 2 | bytes 476269 | solution.py:96
  511.6 16.6 %while.19 = (s32[]{:T(128)}, f32[30,4112]{1,0:T(8,128)S(1)}, s32[6,2]{0,1:T(2,128)S(1)}, f32[6,13,4096]{2,1,0:T(8,128)}, s32[]{:T(128)}) while((s32[]{:T(128)}, f32[30,4112]{1,0:T(8,128)S(1)}, s32[6,2]{0,1:T(2,128)S(1)}, f32[6,13,4096]{2,1,0:T(8,128)}, s32[]{:T(128)}) %tuple.239), condition=%wide.while_cond.8, body=%wide.while_body.8.sunk | while | flops 2 | bytes 476269 | solution.py:96
  528.4 12.5 %while.17 = (s32[]{:T(128)}, f32[30,4112]{1,0:T(8,128)S(1)}, s32[6,2]{0,1:T(2,128)S(1)}, f32[6,13,4096]{2,1,0:T(8,128)S(1)}, s32[]{:T(128)}) while((s32[]{:T(128)}, f32[30,4112]{1,0:T(8,128)S(1)}, s32[6,2]{0,1:T(2,128)S(1)}, f32[6,13,4096]{2,1,0:T(8,128)S(1)}, s32[]{:T(128)}) %tuple.238), condition=%wide.while_cond.6, body=%wide.while_body.6.sunk | while | flops 2 | bytes 524405 | solution.py:96
  543.4 15.9 %while.18 = (s32[]{:T(128)}, f32[30,4112]{1,0:T(8,128)S(1)}, s32[6,2]{0,1:T(2,128)S(1)}, f32[6,13,4096]{2,1,0:T(8,128)}, s32[]{:T(128)}) while((s32[]{:T(128)}, f32[30,4112]{1,0:T(8,128)S(1)}, s32[6,2]{0,1:T(2,128)S(1)}, f32[6,13,4096]{2,1,0:T(8,128)}, s32[]{:T(128)}) %tuple.237), condition=%wide.while_cond.7, body=%wide.while_body.7.sunk | while | flops 2 | bytes 476269 | solution.py:96
  563.9 6.7 collective-permute-start.13
  582.8 7.5 %collective-permute-done.15 = f32[6,8,4096]{2,1,0:T(8,128)S(1)} collective-permute-done((f32[6,8,4096]{2,1,0:T(8,128)S(1)}, f32[6,8,4096]{2,1,0:T(8,128)S(1)}, u32[]{:S(2)}, u32[]{:S(2)}) %collective-permute-start.15) | collective-permute-done | bytes 786464 | tf_op jit(solution)/shard_map/ppermute | solution.py:27
  594.4 22.3 %while.21 = (s32[]{:T(128)}, f32[6,28,4112]{2,1,0:T(8,128)}, s32[6,3]{0,1:T(4,128)S(1)}, f32[6,12,4096]{2,1,0:T(8,128)S(1)}, s32[]{:T(128)}) while((s32[]{:T(128)}, f32[6,28,4112]{2,1,0:T(8,128)}, s32[6,3]{0,1:T(4,128)S(1)}, f32[6,12,4096]{2,1,0:T(8,128)S(1)}, s32[]{:T(128)}) %tuple.236), condition=%wide.while_cond.10, body=%wide.while_body.10.sunk | while | flops 2 | bytes 458889 | solution.py:72
  618.3 80.4 %psum.31 = f32[]{:T(128)} all-reduce(f32[]{:T(128)} %get-tuple-element.182), channel_id=1, replica_groups=mesh['layer'=4,'tile'=64] {'layer','tile'}, use_global_device_ids=true, to_apply=%region_10.11 | all-reduce | flops 1 | bytes 8 | tf_op jit(solution)/shard_map/psum | solution.py:117
  (345 shorter events, 299.1 us)
Async XLA Ops:
  7.2 138.3 %all-gather.3.cloned.1.call-start = ((), (), s32[]{:S(2)}) async-start(), calls=%async_computation | async-start | bytes 2621440 | tf_op jit(solution)/shard_map/all_gather | solution.py:89
  13.1 6.1 collective-permute-start
  21.7 5.9 collective-permute-start.1
  28.8 7.5 %copy-start.19 = (s32[6,4,2]{0,2,1:T(2,128)S(1)}, s32[6,4,2]{0,2,1:T(2,128)}, u32[]{:S(2)}) copy-start(s32[6,4,2]{0,2,1:T(2,128)} %param.6) | copy-start | bytes 580
  30.1 14.2 %collective-permute-start.3 = (f32[6,8,4096]{2,1,0:T(8,128)}, f32[6,8,4096]{2,1,0:T(8,128)S(1)}, u32[]{:S(2)}, u32[]{:S(2)}) collective-permute-start(f32[6,8,4096]{2,1,0:T(8,128)} %get-tuple-element.230), channel_id=1, source_target_pairs={{1,0},{2,1},{3,2},{4,3},{5,4},{6,5},{7,6},{8,7},{9,8},{10,9},{11,1... | collective-permute-start | bytes 2359304 | tf_op jit(solution)/shard_map/ppermute | solution.py:27
  32.0 13.5 %collective-permute-start.2 = (f32[6,8,4096]{2,1,0:T(8,128)}, f32[6,8,4096]{2,1,0:T(8,128)}, u32[]{:S(2)}, u32[]{:S(2)}) collective-permute-start(f32[6,8,4096]{2,1,0:T(8,128)} %get-tuple-element.229), channel_id=1, source_target_pairs={{0,1},{1,2},{2,3},{3,4},{4,5},{5,6},{6,7},{7,8},{8,9},{9,10},{10,1... | collective-permute-start | bytes 2359304 | tf_op jit(solution)/shard_map/ppermute | solution.py:25
  72.0 11.6 %copy-start.20 = (f32[4]{0:T(128)S(1)}, f32[4]{0:T(128)}, u32[]{:S(2)}) copy-start(f32[4]{0:T(128)} %param.7) | copy-start | bytes 52
  72.1 8.4 %collective-permute-start.5 = (f32[1,9,4096]{2,1,0:T(8,128)S(1)}, f32[1,9,4096]{2,1,0:T(8,128)S(1)}, u32[]{:S(2)}, u32[]{:S(2)}) collective-permute-start(f32[1,9,4096]{2,1,0:T(8,128)S(1)} %get-tuple-element.236), channel_id=1, source_target_pairs={{1,0},{2,1},{3,2},{4,3},{5,4},{6,5},{7,6},{8,7},{9,8},{10,9},{11,1... | collective-permute-start | bytes 442376 | tf_op jit(solution)/shard_map/ppermute | solution.py:27
  74.0 7.7 %collective-permute-start.4 = (f32[1,9,4096]{2,1,0:T(8,128)S(1)}, f32[1,9,4096]{2,1,0:T(8,128)S(1)}, u32[]{:S(2)}, u32[]{:S(2)}) collective-permute-start(f32[1,9,4096]{2,1,0:T(8,128)S(1)} %get-tuple-element.235), channel_id=1, source_target_pairs={{0,1},{1,2},{2,3},{3,4},{4,5},{5,6},{6,7},{7,8},{8,9},{9,10},{10,1... | collective-permute-start | bytes 442376 | tf_op jit(solution)/shard_map/ppermute | solution.py:25
  83.3 406.9 %all-gather.5.cloned.1.call-start = ((), (), s32[]{:S(2)}) async-start(), calls=%async_computation.1 | async-start | bytes 2621440 | tf_op jit(solution)/shard_map/all_gather | solution.py:89
  196.5 18.3 %copy-start = (f32[6,13,4096]{2,1,0:T(8,128)S(1)}, f32[6,13,4096]{2,1,0:T(8,128)}, u32[]{:S(2)}) copy-start(f32[6,13,4096]{2,1,0:T(8,128)} %get-tuple-element.41) | copy-start | bytes 3833860
  219.4 9.2 %collective-permute-start.7 = (f32[6,1,4096]{2,1,0:T(1,128)S(1)}, f32[6,1,4096]{2,1,0:T(1,128)S(1)}, u32[]{:S(2)}, u32[]{:S(2)}) collective-permute-start(f32[6,1,4096]{2,1,0:T(1,128)S(1)} %slice.512), channel_id=1, source_target_pairs={{0,1},{1,2},{2,3},{3,4},{4,5},{5,6},{6,7},{7,8},{8,9},{9,10},{10,1... | collective-permute-start | bytes 294920 | tf_op jit(solution)/shard_map/ppermute | solution.py:14
  226.7 3.5 collective-permute-start.6
  231.5 6.6 copy-start.4
  231.5 6.6 copy-start.10
  231.7 14.1 %collective-permute-start.9 = (f32[6,8,4096]{2,1,0:T(8,128)S(1)}, f32[6,8,4096]{2,1,0:T(8,128)S(1)}, u32[]{:S(2)}, u32[]{:S(2)}) collective-permute-start(f32[6,8,4096]{2,1,0:T(8,128)S(1)} %get-tuple-element.228), channel_id=1, source_target_pairs={{1,0},{2,1},{3,2},{4,3},{5,4},{6,5},{7,6},{8,7},{9,8},{10,9},{11,1... | collective-permute-start | bytes 2359304 | tf_op jit(solution)/shard_map/ppermute | solution.py:27
  233.8 13.2 %collective-permute-start.8 = (f32[6,8,4096]{2,1,0:T(8,128)S(1)}, f32[6,8,4096]{2,1,0:T(8,128)S(1)}, u32[]{:S(2)}, u32[]{:S(2)}) collective-permute-start(f32[6,8,4096]{2,1,0:T(8,128)S(1)} %get-tuple-element.227), channel_id=1, source_target_pairs={{0,1},{1,2},{2,3},{3,4},{4,5},{5,6},{6,7},{7,8},{8,9},{9,10},{10,1... | collective-permute-start | bytes 2359304 | tf_op jit(solution)/shard_map/ppermute | solution.py:25
  430.7 7.7 %collective-permute-start.11 = (f32[1,9,4096]{2,1,0:T(8,128)S(1)}, f32[1,9,4096]{2,1,0:T(8,128)S(1)}, u32[]{:S(2)}, u32[]{:S(2)}) collective-permute-start(f32[1,9,4096]{2,1,0:T(8,128)S(1)} %get-tuple-element.234), channel_id=1, source_target_pairs={{1,0},{2,1},{3,2},{4,3},{5,4},{6,5},{7,6},{8,7},{9,8},{10,9},{11,1... | collective-permute-start | bytes 442376 | tf_op jit(solution)/shard_map/ppermute | solution.py:27
  433.3 6.3 collective-permute-start.10
  542.1 17.2 %copy-start.2 = (f32[6,13,4096]{2,1,0:T(8,128)S(1)}, f32[6,13,4096]{2,1,0:T(8,128)}, u32[]{:S(2)}) copy-start(f32[6,13,4096]{2,1,0:T(8,128)} %get-tuple-element.81) | copy-start | bytes 3833860
  563.9 9.2 %collective-permute-start.13 = (f32[6,1,4096]{2,1,0:T(1,128)S(1)}, f32[6,1,4096]{2,1,0:T(1,128)S(1)}, u32[]{:S(2)}, u32[]{:S(2)}) collective-permute-start(f32[6,1,4096]{2,1,0:T(1,128)S(1)} %slice.527), channel_id=1, source_target_pairs={{0,1},{1,2},{2,3},{3,4},{4,5},{5,6},{6,7},{7,8},{8,9},{9,10},{10,1... | collective-permute-start | bytes 294920 | tf_op jit(solution)/shard_map/ppermute | solution.py:14
  571.2 3.5 collective-permute-start.12
  576.2 14.1 %collective-permute-start.15 = (f32[6,8,4096]{2,1,0:T(8,128)S(1)}, f32[6,8,4096]{2,1,0:T(8,128)S(1)}, u32[]{:S(2)}, u32[]{:S(2)}) collective-permute-start(f32[6,8,4096]{2,1,0:T(8,128)S(1)} %get-tuple-element.226), channel_id=1, source_target_pairs={{1,0},{2,1},{3,2},{4,3},{5,4},{6,5},{7,6},{8,7},{9,8},{10,9},{11,1... | collective-permute-start | bytes 2359304 | tf_op jit(solution)/shard_map/ppermute | solution.py:27
  578.3 13.2 %collective-permute-start.14 = (f32[6,8,4096]{2,1,0:T(8,128)S(1)}, f32[6,8,4096]{2,1,0:T(8,128)S(1)}, u32[]{:S(2)}, u32[]{:S(2)}) collective-permute-start(f32[6,8,4096]{2,1,0:T(8,128)S(1)} %get-tuple-element.225), channel_id=1, source_target_pairs={{0,1},{1,2},{2,3},{3,4},{4,5},{5,6},{6,7},{7,8},{8,9},{9,10},{10,1... | collective-permute-start | bytes 2359304 | tf_op jit(solution)/shard_map/ppermute | solution.py:25
  (15 other events, 61.2 us)
Sparse Core Ops, SparseCore 0:
  83.4 61.9 all-gather.2
  440.6 49.5 all-gather.4
where the time goes:
time: 712 us; the launch traced here: 709 us
  blocking collectives  234 us (33%)
  local copies, waits for them, and re-layouts  218 us (31%)
  waiting for transfers between devices  144 us (20%)
  starting transfers between devices  57.4 us (8%)
  other arithmetic  35.1 us (5%)
  between operations  18.5 us (3%)
    gather x198, local copies, waits for them, and re-layouts  190 us
    psum x2, blocking collectives, squares(): return lax.psum(jnp.sum(field * field), ('layer', 'tile'))  154 us
    all_gather x2, waiting for transfers between devices, per_device(): extended = lax.all_gather(apply_extended, 'layer', axis=0, tiled=True)  106 us
    psum x1, blocking collectives, per_device(): alpha = norm_now / lax.psum(jnp.sum(direction * image), ('layer', 'tile'))  80.4 us
    ppermute x5, waiting for transfers between devices, padded_2(): lax.ppermute(head, axis, [((i + 1) % count, i) for i in range(ends)])  26.8 us
    ppermute x6, starting transfers between devices, shifted(): lax.ppermute(value, axis, [(source, source + steps) for source in range(f...  26.1 us
    ppermute x5, starting transfers between devices, padded_2(): lax.ppermute(tail, axis, [(i, (i + 1) % count) for i in range(ends)])  20.5 us
  transfers between devices with their start and end apart: 18, of which 16 were waited for; matrix products, arithmetic and copies ran while one was open for 1% of the time, Pallas kernels for 0%

commit v1 on v0

v1 whole, which is shorter than its diff:
```python
import functools

import jax
import jax.numpy as jnp
from jax import lax
from jax.experimental import pallas as pl
from jax.experimental.pallas import tpu as pltpu
from jax.sharding import PartitionSpec as P

MESH = pl.DeviceIdType.MESH
F32 = jnp.float32
HALO = 8
MARGIN = 64
REACH = 17


def kernel(
    cfg,
    slopes_hbm, mask_hbm, off, reg,
    est_ref, res_ref,
    sl, mki, eb, q0, cb, sib, prv, nxt, ms, mb, x0, x1, pb, qb, lb, ya, tr, arsrc, ar1, ar2,
    in_sem, msend, mrecv, csend, crecv, hsend, hrecv, tsend, trecv, tlocal, asend, arecv,
):
    dirs, lays, tiles, rows, cols, nl = cfg
    two = 2 * rows
    width = cols // (2 * nl)
    at = width // 128
    nt = at + 1
    st = 2 * at + 2
    g1 = 16 if tiles % 16 == 0 else tiles
    hi = tiles // g1
    g2 = nl * hi
    lay = lax.axis_index("layer")
    t = lax.axis_index("tile")
    chip = lax.div(t, 2)
    h = lax.rem(t, 2)
    chips = tiles // 2
    has_prev = chip > 0
    has_next = chip < chips - 1
    prev0 = 2 * chip - 2
    next0 = 2 * chip + 2
    lane = lax.broadcasted_iota(jnp.int32, (8, 128), 1)
    sub = lax.broadcasted_iota(jnp.int32, (8, 128), 0)
    zero = jnp.zeros((8, 128), F32)

    def rdma(src, dst, ss, rs, dev):
        return pltpu.make_async_remote_copy(
            src_ref=src, dst_ref=dst, send_sem=ss, recv_sem=rs, device_id=dev, device_id_type=MESH
        )

    def wait_bytes(ref, sem):
        pltpu.make_async_copy(ref, ref, sem).wait()

    span = 2 * width

    def mask_in(first, count, at_tile):
        src, dst = pl.ds(pl.multiple_of(first, 128), count), pl.ds(128 * at_tile, count)
        return pltpu.make_async_copy(mask_hbm.at[:, src], mki.at[:, dst], in_sem.at[0])

    def slopes_in(first, count, at_tile):
        src, dst = pl.ds(pl.multiple_of(first, 128), count), pl.ds(128 * at_tile, count)
        return pltpu.make_async_copy(slopes_hbm.at[:, :, :, src], sl.at[:, :, :, dst], in_sem.at[1])

    def cases(act):
        @pl.when(lay == 0)
        def _():
            act(0, span + 128, 1)

        @pl.when(lay == nl - 1)
        def _():
            act(span * (nl - 1) - 128, span + 128, 0)

        @pl.when((lay > 0) & (lay < nl - 1))
        def _():
            act(span * lay - 128, span + 256, 0)

    cases(lambda *w: mask_in(*w).start())
    cases(lambda *w: slopes_in(*w).start())

    @pl.when(lay == 0)
    def _():
        mki[:, 0:128] = jnp.zeros((rows, 128), jnp.int32)
        sl[:, :, :, 0:128] = jnp.zeros((dirs, 2, rows, 128), F32)

    @pl.when(lay == nl - 1)
    def _():
        mki[:, 128 * (st - 1) :] = jnp.zeros((rows, 128), jnp.int32)
        sl[:, :, :, 128 * (st - 1) :] = jnp.zeros((dirs, 2, rows, 128), F32)

    prv[...] = jnp.zeros_like(prv)
    sib[...] = jnp.zeros_like(sib)
    mb[...] = jnp.zeros_like(mb)

    @pl.when(jnp.logical_not(has_next))
    def _():
        nxt[...] = jnp.zeros_like(nxt)

    x0[...] = jnp.zeros_like(x0)
    x1[...] = jnp.zeros_like(x1)

    barrier = pltpu.get_barrier_semaphore()

    def greet(dev):
        pl.semaphore_signal(barrier, inc=1, device_id=dev, device_id_type=MESH)

    other = 2 * chip + 1 - h
    greet((lay, other))

    @pl.when(has_prev)
    def _():
        greet((lay, prev0))
        greet((lay, prev0 + 1))

    @pl.when(has_next)
    def _():
        greet((lay, next0))
        greet((lay, next0 + 1))

    def greet_layers(d, c):
        there = lax.rem(lay + d, nl)
        greet((there, 2 * chip))
        greet((there, 2 * chip + 1))
        return c

    lax.fori_loop(1, nl, greet_layers, 0)
    low, high = lax.rem(t, g1), lax.div(t, g1)

    def member1(d):
        return (lay, high * g1 + lax.rem(low + d, g1))

    me2 = lay * hi + high

    def member2(d):
        index = lax.rem(me2 + d, g2)
        return (lax.div(index, hi), lax.rem(index, hi) * g1 + low)

    def greet1(d, c):
        greet(member1(d))
        return c

    def greet2(d, c):
        greet(member2(d))
        return c

    lax.fori_loop(1, g1, greet1, 0)
    lax.fori_loop(1, g2, greet2, 0)

    eb[...] = jnp.zeros_like(eb)
    q0[...] = jnp.zeros_like(q0)
    cb[:, :, :, 0:8, :] = jnp.zeros((2, lays, nt, 8, 128), F32)

    cases(lambda *w: mask_in(*w).wait())
    bands = [slice(0, 8), slice(8, rows)]
    for k in range(2):
        for band in bands:
            turned = [
                pltpu.roll(mki[band, 128 * j : 128 * j + 128].astype(F32), MARGIN + HALO, 1)
                for j in range(at * k, at * k + nt + 1)
            ]
            keep = lane[: band.stop - band.start] < MARGIN + HALO
            for j in range(nt):
                ms[k, j, band, :] = jnp.where(keep, turned[j], turned[j + 1])
    mine = HALO + 1 + rows * h
    for j in range(nt):
        mb[j, pl.ds(mine, rows), :] = ms[h, j, 0:rows, :]
    pl.semaphore_wait(
        barrier,
        1 + 2 * has_prev.astype(jnp.int32) + 2 * has_next.astype(jnp.int32) + 2 * (nl - 1) + (g1 - 1) + (g2 - 1),
    )

    def mask_sib():
        return rdma(
            ms.at[1 - h, :, pl.ds(0, rows)], mb.at[:, pl.ds(mine, rows)], msend.at[0], mrecv.at[0], (lay, other)
        )

    def mask_down(k):
        return rdma(
            ms.at[k, :, pl.ds(rows - HALO - 1, HALO + 1)], mb.at[:, pl.ds(0, HALO + 1)],
            msend.at[1 + k], mrecv.at[1], (lay, next0 + k),
        )

    def mask_up(k):
        return rdma(
            ms.at[k, :, pl.ds(0, HALO)], mb.at[:, pl.ds(HALO + 1 + two, HALO)],
            msend.at[1 + k], mrecv.at[2], (lay, prev0 + k),
        )

    sends_down = has_next & (h == 1)
    sends_up = has_prev & (h == 0)
    mask_sib().start()

    @pl.when(sends_down)
    def _():
        mask_down(0).start()
        mask_down(1).start()

    @pl.when(sends_up)
    def _():
        mask_up(0).start()
        mask_up(1).start()

    cases(lambda *w: slopes_in(*w).wait())
    first_row = rows * t

    def own_adjoint(g, c):
        for band in bands:
            for j in range(st):
                at_cols = slice(128 * j, 128 * j + 128)
                m = mki[band, at_cols].astype(F32)
                u = m * sl[g, 0, band, at_cols]
                w = m * sl[g, 1, band, at_cols]
                eb[0, j, 8 + band.start : 8 + band.stop, :] = u + w
                eb[1, j, 8 + band.start : 8 + band.stop, :] = u - w
        for rb in range(2):
            lo, up = 8 + 8 * rb, 7 + 8 * rb
            row_in = (first_row + 8 * rb + sub < rows * tiles).astype(F32)
            right = []
            for j in range(st):
                right.append(pltpu.roll(eb[0, j, up : up + 8, :] + eb[1, j, lo : lo + 8, :], 1, 1))
            for j in range(st):
                f = jnp.where(lane >= 1, right[j], right[max(j - 1, 0)])
                q = 0.5 * (f - eb[0, j, lo : lo + 8, :] - eb[1, j, up : up + 8, :])
                col_in = (span * lay - 128 + 128 * j + lane < cols).astype(F32)
                q0[g, j, 16 + 8 * rb : 24 + 8 * rb, :] = q * (row_in * col_in)
        return c

    lax.fori_loop(0, dirs, own_adjoint, 0)

    def part_sib(l):
        return rdma(
            cb.at[1 - h, l, :, pl.ds(8, rows + 17)], sib.at[l, :, pl.ds(8, rows + 17)],
            csend.at[l, 0], crecv.at[l, 0], (lay, other),
        )

    def part_down(l, k):
        return rdma(
            cb.at[k, l, :, pl.ds(16 + rows, 9)], prv.at[l, :, pl.ds(0, 9)],
            csend.at[l, 1 + k], crecv.at[l, 1], (lay, next0 + k),
        )

    def part_up(l, k):
        return rdma(
            cb.at[k, l, :, pl.ds(8, 8)], nxt.at[l], csend.at[l, 1 + k], crecv.at[l, 2], (lay, prev0 + k)
        )

    def parts(l, c):
        def block(rb, c):
            total = [[zero] * nt, [zero] * nt]
            for g in range(dirs):
                a, s = off[g, l, 0], MARGIN + off[g, l, 1]
                start = 8 + 8 * rb - a
                turned = [pltpu.roll(q0[g, j, pl.ds(start, 8), :], s, 1) for j in range(st)]
                keep = lane < s
                for k in range(2):
                    for j in range(nt):
                        total[k][j] = total[k][j] + jnp.where(keep, turned[at * k + j], turned[at * k + j + 1])
            for k in range(2):
                for j in range(nt):
                    cb[k, l, j, pl.ds(pl.multiple_of(8 + 8 * rb, 8), 8), :] = total[k][j]
            return c

        lax.fori_loop(0, 4, block, 0)
        part_sib(l).start()

        @pl.when(sends_down)
        def _():
            part_down(l, 0).start()
            part_down(l, 1).start()

        @pl.when(sends_up)
        def _():
            part_up(l, 0).start()
            part_up(l, 1).start()

        return c

    lax.fori_loop(0, lays, parts, 0)

    c0 = width * (2 * lay + h)
    xcol = [c0 - MARGIN + 128 * j + lane for j in range(nt)]
    x_in = [((v >= 0) & (v < cols)).astype(F32) for v in xcol]
    x_own = [((v >= c0) & (v < c0 + width)).astype(F32) for v in xcol]
    pcol = [c0 - MARGIN - HALO + 128 * j + lane for j in range(nt)]
    p_in = [((v >= 0) & (v < cols)).astype(F32) for v in pcol]
    p_own = [((v >= c0) & (v < c0 + width)).astype(F32) for v in pcol]
    chip_row = two * chip

    def row_inside(start):
        r = chip_row + start + sub
        return ((r >= 0) & (r < rows * tiles)).astype(F32)

    def halo_up(x, i, l):
        return rdma(
            x.at[l, :, pl.ds(24, REACH)], x.at[l, :, pl.ds(24 + two, REACH)],
            hsend.at[i, l, 0], hrecv.at[i, l, 0], (lay, prev0 + h),
        )

    def halo_down(x, i, l):
        return rdma(
            x.at[l, :, pl.ds(24 + two - REACH, REACH)], x.at[l, :, pl.ds(24 - REACH, REACH)],
            hsend.at[i, l, 1], hrecv.at[i, l, 1], (lay, next0 + h),
        )

    def send_halo(x, i, l):
        @pl.when(has_prev)
        def _():
            halo_up(x, i, l).start()

        @pl.when(has_next)
        def _():
            halo_down(x, i, l).start()

    def wait_halo(x, i, l):
        @pl.when(has_prev)
        def _():
            halo_down(x, i, l).wait_recv()

        @pl.when(has_next)
        def _():
            halo_up(x, i, l).wait_recv()

    def piece(i, l, half):
        src = ya.at[i, l, :, pl.ds(rows * half, rows)]
        dst = tr.at[i, pl.ds(at * (2 * lay + h), at), pl.ds(0, rows)]
        return src, dst

    def send_pieces(i, l):
        for half in range(2):
            src, dst = piece(i, l, half)
            here = (l == lay) & (half == h)

            @pl.when(here)
            def _():
                pltpu.make_async_copy(src, dst, tlocal.at[i]).start()

            @pl.when(jnp.logical_not(here))
            def _():
                rdma(src, dst, tsend.at[i], trecv.at[i], (l, 2 * chip + half)).start()

    def stage(i, l, rb, value):
        turned = [pltpu.roll(v, MARGIN, 1) for v in value]
        for k in range(at):
            ya[i, l, k, 8 * rb : 8 * rb + 8, :] = jnp.where(lane < MARGIN, turned[k], turned[k + 1])

    def finish_b(l, acc):
        part_sib(l).wait_recv()

        @pl.when(has_prev)
        def _():
            part_down(l, 0).wait_recv()

        @pl.when(has_next)
        def _():
            part_up(l, 0).wait_recv()

        for rb in range(two // 8):
            value = []
            for j in range(nt):
                v = cb[h, l, j, pl.ds(16 + 8 * rb - rows * h, 8), :]
                v = v + sib[l, j, pl.ds(16 + 8 * rb - rows * (1 - h), 8), :]
                if rb < 2:
                    v = v + prv[l, j, 8 * rb : 8 * rb + 8, :]
                if rb == two // 8 - 1:
                    v = v + nxt[l, j]
                v = v * x_in[j]
                acc = acc + x_own[j] * (v * v)
                x0[l, j, 24 + 8 * rb : 32 + 8 * rb, :] = v
                value.append(v)
            stage(0, l, rb, value)
        send_halo(x0, 0, l)
        send_pieces(0, l)
        return acc

    bb = lax.fori_loop(0, lays, finish_b, zero)

    mask_sib().wait_recv()

    @pl.when(has_prev)
    def _():
        mask_down(0).wait_recv()

    @pl.when(has_next)
    def _():
        mask_up(0).wait_recv()

    def beside(value):
        n = len(value)
        r = [pltpu.roll(v, 1, 1) for v in value]
        l = [pltpu.roll(v, 127, 1) for v in value]
        left = [jnp.where(lane >= 1, r[j], r[(j - 1) % n]) for j in range(n)]
        right = [jnp.where(lane < 127, l[j], l[(j + 1) % n]) for j in range(n)]
        return left, right

    def front(x, i):
        def smooth(l, acc):
            wait_halo(x, i, l)
            part = zero
            for rb in range(4):
                row = -1 + 8 * rb
                mid = [x[l, j, 24 + row : 32 + row, :] for j in range(nt)]
                left, right = beside(mid)
                inside = row_inside(row)
                own = ((row + sub >= 0) & (row + sub < two)).astype(F32)
                for j in range(nt):
                    v = 4.0 * mid[j] - x[l, j, 23 + row : 31 + row, :] - x[l, j, 25 + row : 33 + row, :]
                    v = (v - left[j] - right[j]) * (inside * x_in[j])
                    lb[l, j, 8 * rb : 8 * rb + 8, :] = v
                    part = part + (own * x_own[j]) * (v * v)
            return acc + reg[l] * part

        energy = lax.fori_loop(0, lays, smooth, zero)

        def project(g, acc):
            for rb in range(6):
                total = [zero] * nt
                for l in range(lays):
                    a, s = off[g, l, 0], HALO - off[g, l, 1]
                    start = 15 + 8 * rb + a
                    turned = [pltpu.roll(x[l, j, pl.ds(start, 8), :], s, 1) for j in range(nt)]
                    keep = lane >= s
                    total = [total[j] + jnp.where(keep, turned[j], turned[(j - 1) % nt]) for j in range(nt)]
                inside = row_inside(8 * rb - 9)
                total = [total[j] * (inside * p_in[j]) for j in range(nt)]
                turned = [pltpu.roll(v, 127, 1) for v in total]
                for j in range(nt):
                    pb[0, j, 8 * rb : 8 * rb + 8, :] = total[j]
                    pb[1, j, 8 * rb : 8 * rb + 8, :] = jnp.where(lane < 127, turned[j], turned[(j + 1) % nt])
            for rb in range(5):
                up, lo, dn = 8 * rb, 8 * rb + 1, 8 * rb + 2
                turned, rest = [], []
                inside = row_inside(8 * rb - 8)
                for j in range(nt):
                    m_lo, m_up = mb[j, lo : lo + 8, :], mb[j, up : up + 8, :]
                    p_lo, r_lo = pb[0, j, lo : lo + 8, :], pb[1, j, lo : lo + 8, :]
                    e1 = m_lo * (pb[1, j, dn : dn + 8, :] - p_lo)
                    e2 = m_lo * (r_lo - pb[0, j, dn : dn + 8, :])
                    e1_up = m_up * (r_lo - pb[0, j, up : up + 8, :])
                    e2_up = m_up * (pb[1, j, up : up + 8, :] - p_lo)
                    if 1 <= rb <= two // 8:
                        acc = acc + (0.5 * p_own[j]) * (e1 * e1 + e2 * e2)
                    turned.append(pltpu.roll(e1_up + e2, 1, 1))
                    rest.append(e1 + e2_up)
                for j in range(nt):
                    f = jnp.where(lane >= 1, turned[j], turned[(j - 1) % nt])
                    qb[g, j, 8 * rb : 8 * rb + 8, :] = (f - rest[j]) * (0.5 * inside * p_in[j])
            return acc

        return lax.fori_loop(0, dirs, project, energy)

    def back(i, x_next, first, last, acc):
        def layer(l, acc):
            for rb in range(two // 8):
                total = [zero] * nt
                for g in range(dirs):
                    a, s = off[g, l, 0], lax.rem(120 + off[g, l, 1], 128)
                    start = 8 + 8 * rb - a
                    turned = [pltpu.roll(qb[g, j, pl.ds(start, 8), :], s, 1) for j in range(nt)]
                    keep = lane < 120 + off[g, l, 1]
                    total = [total[j] + jnp.where(keep, turned[j], turned[(j + 1) % nt]) for j in range(nt)]
                lo = 8 * rb + 1
                mid = [lb[l, j, lo : lo + 8, :] for j in range(nt)]
                left, right = beside(mid)
                value = []
                for j in range(nt):
                    v = 4.0 * mid[j] - lb[l, j, lo - 1 : lo + 7, :] - lb[l, j, lo + 1 : lo + 9, :] - left[j] - right[j]
                    v = (total[j] + reg[l] * v) * x_in[j]
                    if x_next is not None:
                        acc = acc + x_own[j] * (v * v)
                        x_next[l, j, 24 + 8 * rb : 32 + 8 * rb, :] = v
                    value.append(v)
                stage(i, l, rb, value)
            if x_next is not None:
                send_halo(x_next, 1, l)
            send_pieces(i, l)
            return acc

        return lax.fori_loop(first, last, layer, acc)

    e0 = front(x0, 0)
    yy = back(1, x1, 0, lays, zero)
    e1 = front(x1, 1)

    def rowsum(v):
        return jnp.sum(v, axis=0, keepdims=True)

    packed = jnp.where(
        sub == 0, rowsum(bb), jnp.where(sub == 1, rowsum(e0), jnp.where(sub == 2, rowsum(yy), rowsum(e1)))
    )
    arsrc[0] = packed

    def exchange(stage_id, slots, count, member):
        def one(d, c):
            rdma(arsrc.at[stage_id], slots.at[count - 1 - d], asend.at[stage_id], arecv.at[stage_id], member(d)).start()
            return c

        lax.fori_loop(1, count, one, 0)

    exchange(0, ar1, g1, member1)
    half = (lays + 1) // 2
    back(2, None, 0, half, zero)
    wait_bytes(ar1, arecv.at[0])
    total = arsrc[0]
    for k in range(g1 - 1):
        total = total + ar1[k]
    arsrc[1] = total
    exchange(1, ar2, g2, member2)
    back(2, None, half, lays, zero)
    wait_bytes(ar2, arecv.at[1])
    total = arsrc[1]
    for k in range(g2 - 1):
        total = total + ar2[k]
    sums = jnp.sum(total, axis=1, keepdims=True)
    bb, e0, yy, e1 = (sums[k : k + 1] for k in range(4))
    a0 = bb / e0
    rr = a0 * a0 * yy - bb
    beta = rr / bb
    grown = 1.0 + beta
    a1 = rr / (grown * grown * e0 - 2.0 * a0 * grown * yy + a0 * a0 * e1)
    k0 = a0 + a1 * grown
    k1 = a0 * a1

    for i in range(3):
        wait_bytes(tr.at[i, pl.ds(0, at * (2 * nl - 1)), pl.ds(0, rows)], trecv.at[i])
        src, dst = piece(i, 0, 0)
        pltpu.make_async_copy(src, dst, tlocal.at[i]).wait()

    def write(ct, c):
        out = pl.ds(pl.multiple_of(128 * ct, 128), 128)
        b, y1, y2 = (tr[i, ct, 0:rows, :] for i in range(3))
        est_ref[0, :, out] = k0 * b - k1 * y1
        res_ref[0, :, out] = b - k0 * y1 + k1 * y2
        return c

    lax.fori_loop(0, cols // 128, write, 0, unroll=4)

    mask_sib().wait_send()

    @pl.when(sends_down)
    def _():
        mask_down(0).wait_send()
        mask_down(1).wait_send()

    @pl.when(sends_up)
    def _():
        mask_up(0).wait_send()
        mask_up(1).wait_send()

    def drain(l, c):
        part_sib(l).wait_send()

        @pl.when(sends_down)
        def _():
            part_down(l, 0).wait_send()
            part_down(l, 1).wait_send()

        @pl.when(sends_up)
        def _():
            part_up(l, 0).wait_send()
            part_up(l, 1).wait_send()

        for i, x in enumerate((x0, x1)):

            @pl.when(has_prev)
            def _():
                halo_up(x, i, l).wait_send()

            @pl.when(has_next)
            def _():
                halo_down(x, i, l).wait_send()

        return c

    lax.fori_loop(0, lays, drain, 0)
    for i in range(3):
        wait_bytes(tr.at[i, pl.ds(0, at * (2 * nl - 1)), pl.ds(0, rows)], tsend.at[i])
    wait_bytes(ar1, asend.at[0])
    wait_bytes(ar2, asend.at[1])


def per_device(shape, measured_slopes, valid_mask, layer_offsets, reg_weight):
    nl, tiles = shape
    dirs, _, rows, cols = measured_slopes.shape
    lays = layer_offsets.shape[1]
    width = cols // (2 * nl)
    at = width // 128
    nt, st = at + 1, 2 * at + 2
    g1 = 16 if tiles % 16 == 0 else tiles
    g2 = nl * tiles // g1
    vm = lambda *s: pltpu.VMEM(s, F32)
    dma = lambda *s: pltpu.SemaphoreType.DMA(s)
    out = jax.ShapeDtypeStruct((1, rows, cols), F32)
    return pl.pallas_call(
        functools.partial(kernel, (dirs, lays, tiles, rows, cols, nl)),
        out_shape=(out, out),
        in_specs=[pl.BlockSpec(memory_space=pl.ANY)] * 2 + [pl.BlockSpec(memory_space=pltpu.SMEM)] * 2,
        out_specs=(pl.BlockSpec(memory_space=pltpu.VMEM),) * 2,
        scratch_shapes=[
            vm(dirs, 2, rows, 128 * st),
            pltpu.VMEM((rows, 128 * st), jnp.int32),
            vm(2, st, 32, 128),
            vm(dirs, st, 48, 128),
            vm(2, lays, nt, 40, 128),
            vm(lays, nt, 40, 128),
            vm(lays, nt, 16, 128),
            vm(lays, nt, 8, 128),
            vm(2, nt, 16, 128),
            vm(nt, 56, 128),
            vm(lays, nt, 72, 128),
            vm(lays, nt, 72, 128),
            vm(2, nt, 48, 128),
            vm(dirs, nt, 40, 128),
            vm(lays, nt, 32, 128),
            vm(3, lays, at, 24, 128),
            vm(3, cols // 128, 16, 128),
            vm(2, 8, 128),
            vm(g1 - 1, 8, 128),
            vm(g2 - 1, 8, 128),
            dma(2), dma(3), dma(3), dma(lays, 3), dma(lays, 3), dma(2, lays, 2), dma(2, lays, 2),
            dma(3), dma(3), dma(3), dma(2), dma(2),
        ],
        compiler_params=pltpu.CompilerParams(
            collective_id=0, has_side_effects=True, vmem_limit_bytes=32 * 1024 * 1024
        ),
    )(measured_slopes, valid_mask, layer_offsets, reg_weight)


def solution(mesh):
    return jax.shard_map(
        functools.partial(per_device, (mesh.shape["layer"], mesh.shape["tile"])),
        mesh=mesh,
        in_specs=(P(None, None, "tile", None), P("tile", None), P(), P()),
        out_specs=(P("layer", "tile", None), P("layer", "tile", None)),
        check_vma=False,
    )
```

time: 712 us -> 60.6 us (0.09)
  blocking collectives: 234 us -> 0 us
  local copies, waits for them, and re-layouts: 218 us -> 5.65 us
  waiting for transfers between devices: 144 us -> 0 us
  starting transfers between devices: 57.4 us -> 0 us
  Pallas kernels: 0 us -> 54.2 us
  other arithmetic: 35.1 us -> 0 us
  between operations: 18.5 us -> 0.68 us
    psum x3 -> x0, blocking collectives: 234 us -> none  [the longest x2 154 us: squares(): return lax.psum(jnp.sum(field * field), ('layer', 'tile'))]
    gather x198 -> x0, local copies, waits for them, and re-layouts: 190 us -> none
    all_gather x2 -> x0, waiting for transfers between devices: 106 us -> none  [per_device(): extended = lax.all_gather(apply_extended, 'layer', axis=0, tiled=True)]
    ppermute x16 -> x0, starting transfers between devices: 57.1 us -> none  [the longest x6 26.1 us: shifted(): lax.ppermute(value, axis, [(source, source + steps) for source in range(f...]
    pallas_call x0 -> x1, Pallas kernels: none -> 54.2 us  [per_device(): pl.pallas_call(functools.partial(kernel, (dirs, lays, tiles, rows, cols,...]
    ppermute x16 -> x0, waiting for transfers between devices: 38.2 us -> none  [the longest x5 26.8 us: padded_2(): lax.ppermute(head, axis, [((i + 1) % count, i) for i in range(ends)])]
    mul x11 -> x0, other arithmetic: 13.8 us -> none  [the longest x2 5.63 us: per_device(): apply_phase = apply_phase * inside(0, rows + 1)[None]]
    concatenate x9 -> x0, other arithmetic: 11.2 us -> none  [the longest x5 11.2 us: padded_2(): jnp.concatenate([lax.ppermute(tail, axis, [(i, (i + 1) % count) for i in...]
  transfers between devices with their start and end apart: 18 -> 0, of which waited for: 16 -> 0; matrix products, arithmetic and copies ran while one was open for 1% -> 0% of each run, Pallas kernels for 0% -> 0%
where the time goes in v1:
time: 60.6 us; the launch traced here: 60.5 us
  Pallas kernels  54.2 us (89%)
  local copies, waits for them, and re-layouts  5.65 us (9%)
  between operations  0.68 us (1%)
    pallas_call x1, Pallas kernels, per_device(): pl.pallas_call(functools.partial(kernel, (dirs, lays, tiles, rows, cols,...  54.2 us
    unnamed x6, local copies, waits for them, and re-layouts  3.89 us
    pallas_call x2, local copies, waits for them, and re-layouts, per_device(): pl.pallas_call(functools.partial(kernel, (dirs, lays, tiles, rows, cols,...  1.76 us

profile of v1, /device:TPU:1, one launch (start us, length us, event | category | flops | bytes accessed | tf_op | source)
XLA Modules:
  0.0 60.5 jit_solution(11977575717054120289)
XLA Ops:
  0.6 0.0 copy-start.1
  0.6 0.0 copy-start
  0.7 0.8 %copy.7.off = s32[6,4,2]{2,1,0:T(4,128)S(1)} copy(s32[6,4,2]{0,2,1:T(2,128)} %param.6) | data formatting | bytes 384 | tf_op args[2]
  1.5 3.0 %copy.6.slopes_hbm = f32[6,2,12,4096]{3,2,1,0:T(8,128)S(1)} copy(f32[6,2,12,4096]{3,1,2,0:T(2,128)} %param.4) | data formatting | bytes 4718592 | tf_op args[0]
  4.5 0.0 copy-done.1
  4.5 0.0 copy-done
  4.6 54.2 %shard_map.59 = (f32[1,12,4096]{2,1,0:T(8,128)S(1)}, f32[1,12,4096]{2,1,0:T(8,128)S(1)}) custom-call(f32[6,2,12,4096]{3,2,1,0:T(8,128)S(1)} %copy.6.slopes_hbm, s32[12,4096]{1,0:T(8,128)S(1)} %copy-done, s32[6,4,2]{2,1,0:T(4,128)S(1)} %copy.7.off, f32[4]{0:T(128)S(1)} %copy-done.1), custom_call_target="tpu_custom_call" | custom-call | tf_op jit(solution)/shard_map/pallas_call | solution.py:592
  58.8 0.9 %copy.8 = f32[1,12,4096]{2,0,1:T(1,128)} copy(f32[1,12,4096]{2,1,0:T(8,128)S(1)} %get-tuple-element.2) | data formatting | bytes 393216 | tf_op jit(solution)/shard_map/pallas_call | solution.py:592
  59.6 0.9 %copy.9 = f32[1,12,4096]{2,0,1:T(1,128)} copy(f32[1,12,4096]{2,1,0:T(8,128)S(1)} %get-tuple-element.3) | data formatting | bytes 393216 | tf_op jit(solution)/shard_map/pallas_call | solution.py:592
Async XLA Ops:
  0.6 3.9 %copy-start.1 = (f32[4]{0:T(128)S(1)}, f32[4]{0:T(128)}, u32[]{:S(2)}) copy-start(f32[4]{0:T(128)} %reg.1) | copy-start | bytes 52
  0.6 3.9 %copy-start = (s32[12,4096]{1,0:T(8,128)S(1)}, s32[12,4096]{1,0:T(8,128)}, u32[]{:S(2)}) copy-start(s32[12,4096]{1,0:T(8,128)} %mask_hbm.1) | copy-start | bytes 589828

commit v2 on v1

--- a/solution.py
+++ b/solution.py
@@ -58,8 +58,17 @@
         return pltpu.make_async_copy(mask_hbm.at[:, src], mki.at[:, dst], in_sem.at[0])
 
     def slopes_in(first, count, at_tile):
-        src, dst = pl.ds(pl.multiple_of(first, 128), count), pl.ds(128 * at_tile, count)
-        return pltpu.make_async_copy(slopes_hbm.at[:, :, :, src], sl.at[:, :, :, dst], in_sem.at[1])
+        src, dst = pl.ds(lax.div(first, 64), count // 64), pl.ds(2 * at_tile, count // 64)
+
+        def one(i, c):
+            pltpu.make_async_copy(slopes_hbm.at[:, i, src], sl.at[:, dst, i], in_sem.at[1]).start()
+            return c
+
+        lax.fori_loop(0, rows, one, 0)
+
+    def slopes_wait(first, count, at_tile):
+        dst = sl.at[:, pl.ds(2 * at_tile, count // 64), pl.ds(0, rows)]
+        pltpu.make_async_copy(dst, dst, in_sem.at[1]).wait()
 
     def cases(act):
         @pl.when(lay == 0)
@@ -75,17 +84,17 @@
             act(span * lay - 128, span + 256, 0)
 
     cases(lambda *w: mask_in(*w).start())
-    cases(lambda *w: slopes_in(*w).start())
+    cases(slopes_in)
 
     @pl.when(lay == 0)
     def _():
         mki[:, 0:128] = jnp.zeros((rows, 128), jnp.int32)
-        sl[:, :, :, 0:128] = jnp.zeros((dirs, 2, rows, 128), F32)
+        sl[:, 0:2, 0:rows] = jnp.zeros((dirs, 2, rows, 128), F32)
 
     @pl.when(lay == nl - 1)
     def _():
         mki[:, 128 * (st - 1) :] = jnp.zeros((rows, 128), jnp.int32)
-        sl[:, :, :, 128 * (st - 1) :] = jnp.zeros((dirs, 2, rows, 128), F32)
+        sl[:, 2 * st - 2 :, 0:rows] = jnp.zeros((dirs, 2, rows, 128), F32)
 
     prv[...] = jnp.zeros_like(prv)
     sib[...] = jnp.zeros_like(sib)
@@ -199,7 +208,7 @@
         mask_up(0).start()
         mask_up(1).start()
 
-    cases(lambda *w: slopes_in(*w).wait())
+    cases(slopes_wait)
     first_row = rows * t
 
     def own_adjoint(g, c):
@@ -207,8 +216,8 @@
             for j in range(st):
                 at_cols = slice(128 * j, 128 * j + 128)
                 m = mki[band, at_cols].astype(F32)
-                u = m * sl[g, 0, band, at_cols]
-                w = m * sl[g, 1, band, at_cols]
+                u = m * sl[g, 2 * j, band, :]
+                w = m * sl[g, 2 * j + 1, band, :]
                 eb[0, j, 8 + band.start : 8 + band.stop, :] = u + w
                 eb[1, j, 8 + band.start : 8 + band.stop, :] = u - w
         for rb in range(2):
@@ -247,7 +256,7 @@
         def block(rb, c):
             total = [[zero] * nt, [zero] * nt]
             for g in range(dirs):
-                a, s = off[g, l, 0], MARGIN + off[g, l, 1]
+                a, s = off[l, 0, g], MARGIN + off[l, 1, g]
                 start = 8 + 8 * rb - a
                 turned = [pltpu.roll(q0[g, j, pl.ds(start, 8), :], s, 1) for j in range(st)]
                 keep = lane < s
@@ -320,8 +329,8 @@
             halo_up(x, i, l).wait_recv()
 
     def piece(i, l, half):
-        src = ya.at[i, l, :, pl.ds(rows * half, rows)]
-        dst = tr.at[i, pl.ds(at * (2 * lay + h), at), pl.ds(0, rows)]
+        src = ya.at[i, l, pl.ds(at * rows * half, at * rows)].reshape(rows, at, 128)
+        dst = tr.at[i, :, pl.ds(at * (2 * lay + h), at)]
         return src, dst
 
     def send_pieces(i, l):
@@ -340,7 +349,7 @@
     def stage(i, l, rb, value):
         turned = [pltpu.roll(v, MARGIN, 1) for v in value]
         for k in range(at):
-            ya[i, l, k, 8 * rb : 8 * rb + 8, :] = jnp.where(lane < MARGIN, turned[k], turned[k + 1])
+            ya[i, l, pl.ds(at * 8 * rb + k, 8, stride=at), :] = jnp.where(lane < MARGIN, turned[k], turned[k + 1])
 
     def finish_b(l, acc):
         part_sib(l).wait_recv()
@@ -414,7 +423,7 @@
             for rb in range(6):
                 total = [zero] * nt
                 for l in range(lays):
-                    a, s = off[g, l, 0], HALO - off[g, l, 1]
+                    a, s = off[l, 0, g], HALO - off[l, 1, g]
                     start = 15 + 8 * rb + a
                     turned = [pltpu.roll(x[l, j, pl.ds(start, 8), :], s, 1) for j in range(nt)]
                     keep = lane >= s
@@ -452,10 +461,10 @@
             for rb in range(two // 8):
                 total = [zero] * nt
                 for g in range(dirs):
-                    a, s = off[g, l, 0], lax.rem(120 + off[g, l, 1], 128)
+                    a, s = off[l, 0, g], lax.rem(120 + off[l, 1, g], 128)
                     start = 8 + 8 * rb - a
                     turned = [pltpu.roll(qb[g, j, pl.ds(start, 8), :], s, 1) for j in range(nt)]
-                    keep = lane < 120 + off[g, l, 1]
+                    keep = lane < 120 + off[l, 1, g]
                     total = [total[j] + jnp.where(keep, turned[j], turned[(j + 1) % nt]) for j in range(nt)]
                 lo = 8 * rb + 1
                 mid = [lb[l, j, lo : lo + 8, :] for j in range(nt)]
@@ -520,18 +529,18 @@
     k1 = a0 * a1
 
     for i in range(3):
-        wait_bytes(tr.at[i, pl.ds(0, at * (2 * nl - 1)), pl.ds(0, rows)], trecv.at[i])
+        wait_bytes(tr.at[i, :, pl.ds(0, at * (2 * nl - 1))], trecv.at[i])
         src, dst = piece(i, 0, 0)
         pltpu.make_async_copy(src, dst, tlocal.at[i]).wait()
 
-    def write(ct, c):
-        out = pl.ds(pl.multiple_of(128 * ct, 128), 128)
-        b, y1, y2 = (tr[i, ct, 0:rows, :] for i in range(3))
-        est_ref[0, :, out] = k0 * b - k1 * y1
-        res_ref[0, :, out] = b - k0 * y1 + k1 * y2
+    def write(r, c):
+        for ct in range(0, cols // 128, 8):
+            b, y1, y2 = (tr[i, r, ct : ct + 8, :] for i in range(3))
+            est_ref[r, ct : ct + 8, :] = k0 * b - k1 * y1
+            res_ref[r, ct : ct + 8, :] = b - k0 * y1 + k1 * y2
         return c
 
-    lax.fori_loop(0, cols // 128, write, 0, unroll=4)
+    lax.fori_loop(0, rows, write, 0, unroll=2)
 
     mask_sib().wait_send()
 
@@ -572,7 +581,7 @@
 
     lax.fori_loop(0, lays, drain, 0)
     for i in range(3):
-        wait_bytes(tr.at[i, pl.ds(0, at * (2 * nl - 1)), pl.ds(0, rows)], tsend.at[i])
+        wait_bytes(tr.at[i, :, pl.ds(0, at * (2 * nl - 1))], tsend.at[i])
     wait_bytes(ar1, asend.at[0])
     wait_bytes(ar2, asend.at[1])
 
@@ -588,14 +597,16 @@
     g2 = nl * tiles // g1
     vm = lambda *s: pltpu.VMEM(s, F32)
     dma = lambda *s: pltpu.SemaphoreType.DMA(s)
-    out = jax.ShapeDtypeStruct((1, rows, cols), F32)
-    return pl.pallas_call(
+    out = jax.ShapeDtypeStruct((rows, cols // 128, 128), F32)
+    slopes = measured_slopes.reshape(dirs, 2, rows, cols // 128, 128).transpose(0, 2, 3, 1, 4)
+    slopes = slopes.reshape(dirs, rows, cols // 64, 128)
+    est, res = pl.pallas_call(
         functools.partial(kernel, (dirs, lays, tiles, rows, cols, nl)),
         out_shape=(out, out),
-        in_specs=[pl.BlockSpec(memory_space=pl.ANY)] * 2 + [pl.BlockSpec(memory_space=pltpu.SMEM)] * 2,
+        in_specs=[pl.BlockSpec(memory_space=pltpu.HBM)] * 2 + [pl.BlockSpec(memory_space=pltpu.SMEM)] * 2,
         out_specs=(pl.BlockSpec(memory_space=pltpu.VMEM),) * 2,
         scratch_shapes=[
-            vm(dirs, 2, rows, 128 * st),
+            vm(dirs, 2 * st, rows + 4, 128),
             pltpu.VMEM((rows, 128 * st), jnp.int32),
             vm(2, st, 32, 128),
             vm(dirs, st, 48, 128),
@@ -610,8 +621,8 @@
             vm(2, nt, 48, 128),
             vm(dirs, nt, 40, 128),
             vm(lays, nt, 32, 128),
-            vm(3, lays, at, 24, 128),
-            vm(3, cols // 128, 16, 128),
+            vm(3, lays, at * 2 * rows, 128),
+            vm(3, rows, cols // 128, 128),
             vm(2, 8, 128),
             vm(g1 - 1, 8, 128),
             vm(g2 - 1, 8, 128),
@@ -619,9 +630,10 @@
             dma(3), dma(3), dma(3), dma(2), dma(2),
         ],
         compiler_params=pltpu.CompilerParams(
-            collective_id=0, has_side_effects=True, vmem_limit_bytes=32 * 1024 * 1024
+            collective_id=0, has_side_effects=True, vmem_limit_bytes=56 * 1024 * 1024
         ),
-    )(measured_slopes, valid_mask, layer_offsets, reg_weight)
+    )(slopes, valid_mask, layer_offsets.transpose(1, 2, 0), reg_weight)
+    return est.reshape(1, rows, cols), res.reshape(1, rows, cols)
 
 
 def solution(mesh):

time: 60.6 us -> 58.8 us (0.970)
  local copies, waits for them, and re-layouts: 5.65 us -> 3.23 us
    pallas_call x2 -> x0, local copies, waits for them, and re-layouts: 1.76 us -> none  [per_device(): pl.pallas_call(functools.partial(kernel, (dirs, lays, tiles, rows, cols,...]
    unnamed x6 -> x2, local copies, waits for them, and re-layouts: 3.89 us -> 3.23 us
    pallas_call x1, Pallas kernels: 54.2 us -> 54.8 us  [per_device(): pl.pallas_call(functools.partial(kernel, (dirs, lays, tiles, rows, cols,...]
where the time goes in v2:
time: 58.8 us; the launch traced here: 58.7 us
  Pallas kernels  54.8 us (93%)
  local copies, waits for them, and re-layouts  3.23 us (5%)
  between operations  0.64 us (1%)
    pallas_call x1, Pallas kernels, per_device(): pl.pallas_call(functools.partial(kernel, (dirs, lays, tiles, rows, cols,...  54.8 us
    unnamed x2, local copies, waits for them, and re-layouts  3.23 us

profile of v2, /device:TPU:1, one launch (start us, length us, event | category | flops | bytes accessed | tf_op | source)
XLA Modules:
  0.0 58.7 jit_solution(3692115101129750627)
XLA Ops:
  0.6 54.8 %shard_map.59 = (f32[12,32,128]{2,1,0:T(8,128)}, f32[12,32,128]{2,1,0:T(8,128)}) custom-call(f32[6,12,64,128]{3,2,1,0:T(8,128)} %bitcast.8, s32[12,4096]{1,0:T(8,128)} %mask_hbm.1, s32[4,2,6]{2,1,0:T(2,128)} %bitcast.11, f32[4]{0:T(128)} %reg.1), custom_call_target="tpu_custom_call" | custom-call | tf_op jit(solution)/shard_map/pallas_call | solution.py:603
  55.4 1.6 %copy.14 = f32[1,12,4096]{2,0,1:T(1,128)} copy(f32[1,12,4096]{2,0,1:T(1,128)} %bitcast.10) | data formatting | bytes 393216
  57.0 1.6 %copy.15 = f32[1,12,4096]{2,0,1:T(1,128)} copy(f32[1,12,4096]{2,0,1:T(1,128)} %bitcast.9) | data formatting | bytes 393216

commit v3 on v2

--- a/solution.py
+++ b/solution.py
@@ -17,19 +17,20 @@
 def kernel(
     cfg,
     slopes_hbm, mask_hbm, off, reg,
-    est_ref, res_ref,
-    sl, mki, eb, q0, cb, sib, prv, nxt, ms, mb, x0, x1, pb, qb, lb, ya, tr, arsrc, ar1, ar2,
+    b_out, y1_out, y2_out, k0_ref, k1_ref,
+    sl, mki, eb, q0, cb, sib, prv, nxt, ms, mb, x0, x1, pb, qb, lb, ya, arsrc, ar1, ar2,
     in_sem, msend, mrecv, csend, crecv, hsend, hrecv, tsend, trecv, tlocal, asend, arecv,
 ):
     dirs, lays, tiles, rows, cols, nl = cfg
     two = 2 * rows
+    outs = (b_out, y1_out, y2_out)
     width = cols // (2 * nl)
     at = width // 128
     nt = at + 1
     st = 2 * at + 2
-    g1 = 16 if tiles % 16 == 0 else tiles
-    hi = tiles // g1
-    g2 = nl * hi
+    zs, xs = (2, 4) if tiles % 16 == 0 else (1, tiles // 2)
+    g1 = nl * zs * 2
+    g2 = tiles // (zs * 2)
     lay = lax.axis_index("layer")
     t = lax.axis_index("tile")
     chip = lax.div(t, 2)
@@ -132,16 +133,21 @@
         return c
 
     lax.fori_loop(1, nl, greet_layers, 0)
-    low, high = lax.rem(t, g1), lax.div(t, g1)
+    tx, tz, ty = lax.rem(chip, xs), lax.rem(lax.div(chip, xs), zs), lax.div(chip, xs * zs)
+    me1 = (lay * zs + tz) * 2 + h
+    me2 = ty * xs + tx
+
+    def tile_at(y, z, x, core):
+        return ((y * zs + z) * xs + x) * 2 + core
 
     def member1(d):
-        return (lay, high * g1 + lax.rem(low + d, g1))
-
-    me2 = lay * hi + high
+        index = lax.rem(me1 + d, g1)
+        there = lax.div(index, 2 * zs)
+        return (there, tile_at(ty, lax.rem(lax.div(index, 2), zs), tx, lax.rem(index, 2)))
 
     def member2(d):
         index = lax.rem(me2 + d, g2)
-        return (lax.div(index, hi), lax.rem(index, hi) * g1 + low)
+        return (lay, tile_at(lax.div(index, xs), tz, lax.rem(index, xs), h))
 
     def greet1(d, c):
         greet(member1(d))
@@ -330,7 +336,7 @@
 
     def piece(i, l, half):
         src = ya.at[i, l, pl.ds(at * rows * half, at * rows)].reshape(rows, at, 128)
-        dst = tr.at[i, :, pl.ds(at * (2 * lay + h), at)]
+        dst = outs[i].at[:, pl.ds(at * (2 * lay + h), at)]
         return src, dst
 
     def send_pieces(i, l):
@@ -377,7 +383,6 @@
                 value.append(v)
             stage(0, l, rb, value)
         send_halo(x0, 0, l)
-        send_pieces(0, l)
         return acc
 
     bb = lax.fori_loop(0, lays, finish_b, zero)
@@ -418,6 +423,12 @@
             return acc + reg[l] * part
 
         energy = lax.fori_loop(0, lays, smooth, zero)
+
+        def give(l, c):
+            send_pieces(i, l)
+            return c
+
+        lax.fori_loop(0, lays, give, 0)
 
         def project(g, acc):
             for rb in range(6):
@@ -480,7 +491,8 @@
                 stage(i, l, rb, value)
             if x_next is not None:
                 send_halo(x_next, 1, l)
-            send_pieces(i, l)
+            else:
+                send_pieces(i, l)
             return acc
 
         return lax.fori_loop(first, last, layer, acc)
@@ -489,58 +501,46 @@
     yy = back(1, x1, 0, lays, zero)
     e1 = front(x1, 1)
 
-    def rowsum(v):
-        return jnp.sum(v, axis=0, keepdims=True)
-
-    packed = jnp.where(
-        sub == 0, rowsum(bb), jnp.where(sub == 1, rowsum(e0), jnp.where(sub == 2, rowsum(yy), rowsum(e1)))
-    )
-    arsrc[0] = packed
+    lane1 = lane[0:1]
+
+    def whole(v):
+        return jnp.sum(jnp.sum(v, axis=0, keepdims=True), axis=1, keepdims=True)
+
+    packed = jnp.zeros((1, 128), F32)
+    for k, v in enumerate((bb, e0, yy, e1)):
+        packed = jnp.where(lane1 == k, whole(v), packed)
+    arsrc[0:1, :] = packed
 
     def exchange(stage_id, slots, count, member):
         def one(d, c):
-            rdma(arsrc.at[stage_id], slots.at[count - 1 - d], asend.at[stage_id], arecv.at[stage_id], member(d)).start()
+            rdma(
+                arsrc.at[pl.ds(8 * stage_id, 1)], slots.at[pl.ds(count - 1 - d, 1)],
+                asend.at[stage_id], arecv.at[stage_id], member(d),
+            ).start()
             return c
 
         lax.fori_loop(1, count, one, 0)
 
     exchange(0, ar1, g1, member1)
-    half = (lays + 1) // 2
-    back(2, None, 0, half, zero)
+    back(2, None, 0, lays, zero)
     wait_bytes(ar1, arecv.at[0])
-    total = arsrc[0]
-    for k in range(g1 - 1):
-        total = total + ar1[k]
-    arsrc[1] = total
+    arsrc[8:9, :] = arsrc[0:1, :] + jnp.sum(ar1[...], axis=0, keepdims=True)
     exchange(1, ar2, g2, member2)
-    back(2, None, half, lays, zero)
     wait_bytes(ar2, arecv.at[1])
-    total = arsrc[1]
-    for k in range(g2 - 1):
-        total = total + ar2[k]
-    sums = jnp.sum(total, axis=1, keepdims=True)
-    bb, e0, yy, e1 = (sums[k : k + 1] for k in range(4))
+    total = arsrc[8:9, :] + jnp.sum(ar2[...], axis=0, keepdims=True)
+    bb, e0, yy, e1 = (jnp.sum(jnp.where(lane1 == k, total, 0.0), axis=1, keepdims=True) for k in range(4))
     a0 = bb / e0
     rr = a0 * a0 * yy - bb
     beta = rr / bb
     grown = 1.0 + beta
     a1 = rr / (grown * grown * e0 - 2.0 * a0 * grown * yy + a0 * a0 * e1)
-    k0 = a0 + a1 * grown
-    k1 = a0 * a1
+    k0_ref[...] = jnp.broadcast_to(a0 + a1 * grown, (1, 128))
+    k1_ref[...] = jnp.broadcast_to(a0 * a1, (1, 128))
 
     for i in range(3):
-        wait_bytes(tr.at[i, :, pl.ds(0, at * (2 * nl - 1))], trecv.at[i])
+        wait_bytes(outs[i].at[:, pl.ds(0, at * (2 * nl - 1))], trecv.at[i])
         src, dst = piece(i, 0, 0)
         pltpu.make_async_copy(src, dst, tlocal.at[i]).wait()
-
-    def write(r, c):
-        for ct in range(0, cols // 128, 8):
-            b, y1, y2 = (tr[i, r, ct : ct + 8, :] for i in range(3))
-            est_ref[r, ct : ct + 8, :] = k0 * b - k1 * y1
-            res_ref[r, ct : ct + 8, :] = b - k0 * y1 + k1 * y2
-        return c
-
-    lax.fori_loop(0, rows, write, 0, unroll=2)
 
     mask_sib().wait_send()
 
@@ -581,7 +581,7 @@
 
     lax.fori_loop(0, lays, drain, 0)
     for i in range(3):
-        wait_bytes(tr.at[i, :, pl.ds(0, at * (2 * nl - 1))], tsend.at[i])
+        wait_bytes(outs[i].at[:, pl.ds(0, at * (2 * nl - 1))], tsend.at[i])
     wait_bytes(ar1, asend.at[0])
     wait_bytes(ar2, asend.at[1])
 
@@ -593,18 +593,18 @@
     width = cols // (2 * nl)
     at = width // 128
     nt, st = at + 1, 2 * at + 2
-    g1 = 16 if tiles % 16 == 0 else tiles
-    g2 = nl * tiles // g1
+    zs = 2 if tiles % 16 == 0 else 1
+    g1, g2 = nl * zs * 2, tiles // (zs * 2)
     vm = lambda *s: pltpu.VMEM(s, F32)
     dma = lambda *s: pltpu.SemaphoreType.DMA(s)
     out = jax.ShapeDtypeStruct((rows, cols // 128, 128), F32)
     slopes = measured_slopes.reshape(dirs, 2, rows, cols // 128, 128).transpose(0, 2, 3, 1, 4)
     slopes = slopes.reshape(dirs, rows, cols // 64, 128)
-    est, res = pl.pallas_call(
+    b, y1, y2, k0, k1 = pl.pallas_call(
         functools.partial(kernel, (dirs, lays, tiles, rows, cols, nl)),
-        out_shape=(out, out),
+        out_shape=(out,) * 3 + (jax.ShapeDtypeStruct((1, 128), F32),) * 2,
         in_specs=[pl.BlockSpec(memory_space=pltpu.HBM)] * 2 + [pl.BlockSpec(memory_space=pltpu.SMEM)] * 2,
-        out_specs=(pl.BlockSpec(memory_space=pltpu.VMEM),) * 2,
+        out_specs=(pl.BlockSpec(memory_space=pltpu.HBM),) * 3 + (pl.BlockSpec(memory_space=pltpu.VMEM),) * 2,
         scratch_shapes=[
             vm(dirs, 2 * st, rows + 4, 128),
             pltpu.VMEM((rows, 128 * st), jnp.int32),
@@ -622,10 +622,9 @@
             vm(dirs, nt, 40, 128),
             vm(lays, nt, 32, 128),
             vm(3, lays, at * 2 * rows, 128),
-            vm(3, rows, cols // 128, 128),
-            vm(2, 8, 128),
-            vm(g1 - 1, 8, 128),
-            vm(g2 - 1, 8, 128),
+            vm(16, 128),
+            vm(g1 - 1, 128),
+            vm(g2 - 1, 128),
             dma(2), dma(3), dma(3), dma(lays, 3), dma(lays, 3), dma(2, lays, 2), dma(2, lays, 2),
             dma(3), dma(3), dma(3), dma(2), dma(2),
         ],
@@ -633,6 +632,8 @@
             collective_id=0, has_side_effects=True, vmem_limit_bytes=56 * 1024 * 1024
         ),
     )(slopes, valid_mask, layer_offsets.transpose(1, 2, 0), reg_weight)
+    est = k0 * b - k1 * y1
+    res = b - k0 * y1 + k1 * y2
     return est.reshape(1, rows, cols), res.reshape(1, rows, cols)
 
 

time: 58.8 us -> 51.3 us (0.87)
  Pallas kernels: 54.8 us -> 48.5 us
  local copies, waits for them, and re-layouts: 3.23 us -> 0 us
  other arithmetic: 0 us -> 1.93 us
    pallas_call x1, Pallas kernels: 54.8 us -> 48.5 us  [per_device(): pl.pallas_call(functools.partial(kernel, (dirs, lays, tiles, rows, cols,...]
    unnamed x2 -> x0, local copies, waits for them, and re-layouts: 3.23 us -> none
    add x0 -> x1, other arithmetic: none -> 1.93 us  [per_device(): res = b - k0 * y1 + k1 * y2]
where the time goes in v3:
time: 51.3 us; the launch traced here: 51.1 us
  Pallas kernels  48.5 us (95%)
  other arithmetic  1.93 us (4%)
  between operations  0.64 us (1%)
    pallas_call x1, Pallas kernels, per_device(): pl.pallas_call(functools.partial(kernel, (dirs, lays, tiles, rows, cols,...  48.5 us
    add x1, other arithmetic, per_device(): res = b - k0 * y1 + k1 * y2  1.93 us

profile of v3, /device:TPU:1, one launch (start us, length us, event | category | flops | bytes accessed | tf_op | source)
XLA Modules:
  0.0 51.1 jit_solution(2416412314319132905)
XLA Ops:
  0.6 48.5 %shard_map.59 = (f32[12,32,128]{2,1,0:T(8,128)}, f32[12,32,128]{2,1,0:T(8,128)}, f32[12,32,128]{2,1,0:T(8,128)}, f32[1,128]{1,0:T(1,128)}, f32[1,128]{1,0:T(1,128)}) custom-call(f32[6,12,64,128]{3,2,1,0:T(8,128)} %bitcast.10, s32[12,4096]{1,0:T(8,128)} %mask_hbm.1, s32[4,2,6]{2,1,0:T(2,128)} %bitcast.13, f32[4]{0:T(128)} %reg.1), custom_call_target="tpu_custom_call" | custom-call | tf_op jit(solution)/shard_map/pallas_call | solution.py:603
  49.2 1.9 %multiply_add_fusion = (f32[12,32,128]{2,1,0:T(8,128)}, f32[12,32,128]{2,1,0:T(8,128)}) fusion(f32[12,32,128]{2,1,0:T(8,128)} %get-tuple-element.11, f32[12,32,128]{2,1,0:T(8,128)} %get-tuple-element.8, f32[12,32,128]{2,1,0:T(8,128)} %get-tuple-element.10, f32[128]{0:T(128)} %bitcast.15, f32[128]{0:T(128)} %bitcast.14), kind=kLoop, calls=%fused_computation | loop fusion | flops 344064 | bytes 984064 | tf_op jit(solution)/shard_map/add | solution.py:636

commit v4 on v3

--- a/solution.py
+++ b/solution.py
@@ -11,19 +11,19 @@
 F32 = jnp.float32
 HALO = 8
 MARGIN = 64
+ITERS = 2
 REACH = 17
 
 
 def kernel(
     cfg,
     slopes_hbm, mask_hbm, off, reg,
-    b_out, y1_out, y2_out, k0_ref, k1_ref,
-    sl, mki, eb, q0, cb, sib, prv, nxt, ms, mb, x0, x1, pb, qb, lb, ya, arsrc, ar1, ar2,
+    fields, k0_ref, k1_ref,
+    sl, mki, eb, q0, cb, sib, prv, nxt, ms, mb, xb, xw, sums, pb, qb, lb, ya, arsrc, ar1, ar2,
     in_sem, msend, mrecv, csend, crecv, hsend, hrecv, tsend, trecv, tlocal, asend, arecv,
 ):
     dirs, lays, tiles, rows, cols, nl = cfg
     two = 2 * rows
-    outs = (b_out, y1_out, y2_out)
     width = cols // (2 * nl)
     at = width // 128
     nt = at + 1
@@ -52,69 +52,12 @@
     def wait_bytes(ref, sem):
         pltpu.make_async_copy(ref, ref, sem).wait()
 
-    span = 2 * width
-
-    def mask_in(first, count, at_tile):
-        src, dst = pl.ds(pl.multiple_of(first, 128), count), pl.ds(128 * at_tile, count)
-        return pltpu.make_async_copy(mask_hbm.at[:, src], mki.at[:, dst], in_sem.at[0])
-
-    def slopes_in(first, count, at_tile):
-        src, dst = pl.ds(lax.div(first, 64), count // 64), pl.ds(2 * at_tile, count // 64)
-
-        def one(i, c):
-            pltpu.make_async_copy(slopes_hbm.at[:, i, src], sl.at[:, dst, i], in_sem.at[1]).start()
-            return c
-
-        lax.fori_loop(0, rows, one, 0)
-
-    def slopes_wait(first, count, at_tile):
-        dst = sl.at[:, pl.ds(2 * at_tile, count // 64), pl.ds(0, rows)]
-        pltpu.make_async_copy(dst, dst, in_sem.at[1]).wait()
-
-    def cases(act):
-        @pl.when(lay == 0)
-        def _():
-            act(0, span + 128, 1)
-
-        @pl.when(lay == nl - 1)
-        def _():
-            act(span * (nl - 1) - 128, span + 128, 0)
-
-        @pl.when((lay > 0) & (lay < nl - 1))
-        def _():
-            act(span * lay - 128, span + 256, 0)
-
-    cases(lambda *w: mask_in(*w).start())
-    cases(slopes_in)
-
-    @pl.when(lay == 0)
-    def _():
-        mki[:, 0:128] = jnp.zeros((rows, 128), jnp.int32)
-        sl[:, 0:2, 0:rows] = jnp.zeros((dirs, 2, rows, 128), F32)
-
-    @pl.when(lay == nl - 1)
-    def _():
-        mki[:, 128 * (st - 1) :] = jnp.zeros((rows, 128), jnp.int32)
-        sl[:, 2 * st - 2 :, 0:rows] = jnp.zeros((dirs, 2, rows, 128), F32)
-
-    prv[...] = jnp.zeros_like(prv)
-    sib[...] = jnp.zeros_like(sib)
-    mb[...] = jnp.zeros_like(mb)
-
-    @pl.when(jnp.logical_not(has_next))
-    def _():
-        nxt[...] = jnp.zeros_like(nxt)
-
-    x0[...] = jnp.zeros_like(x0)
-    x1[...] = jnp.zeros_like(x1)
-
     barrier = pltpu.get_barrier_semaphore()
 
     def greet(dev):
         pl.semaphore_signal(barrier, inc=1, device_id=dev, device_id_type=MESH)
 
     other = 2 * chip + 1 - h
-    greet((lay, other))
 
     @pl.when(has_prev)
     def _():
@@ -126,13 +69,6 @@
         greet((lay, next0))
         greet((lay, next0 + 1))
 
-    def greet_layers(d, c):
-        there = lax.rem(lay + d, nl)
-        greet((there, 2 * chip))
-        greet((there, 2 * chip + 1))
-        return c
-
-    lax.fori_loop(1, nl, greet_layers, 0)
     tx, tz, ty = lax.rem(chip, xs), lax.rem(lax.div(chip, xs), zs), lax.div(chip, xs * zs)
     me1 = (lay * zs + tz) * 2 + h
     me2 = ty * xs + tx
@@ -160,8 +96,72 @@
     lax.fori_loop(1, g1, greet1, 0)
     lax.fori_loop(1, g2, greet2, 0)
 
-    eb[...] = jnp.zeros_like(eb)
-    q0[...] = jnp.zeros_like(q0)
+    span = 2 * width
+
+    def mask_in(first, count, at_tile):
+        src, dst = pl.ds(pl.multiple_of(first, 128), count), pl.ds(128 * at_tile, count)
+        return pltpu.make_async_copy(mask_hbm.at[:, src], mki.at[:, dst], in_sem.at[0])
+
+    def slopes_in(first, count, at_tile):
+        src, dst = pl.ds(lax.div(first, 64), count // 64), pl.ds(2 * at_tile, count // 64)
+
+        def one(i, c):
+            pltpu.make_async_copy(slopes_hbm.at[:, i, src], sl.at[:, dst, i], in_sem.at[1]).start()
+            return c
+
+        lax.fori_loop(0, rows, one, 0)
+
+    def slopes_wait(first, count, at_tile):
+        dst = sl.at[:, pl.ds(2 * at_tile, count // 64), pl.ds(0, rows)]
+        pltpu.make_async_copy(dst, dst, in_sem.at[1]).wait()
+
+    def cases(act):
+        @pl.when(lay == 0)
+        def _():
+            act(0, span + 128, 1)
+
+        @pl.when(lay == nl - 1)
+        def _():
+            act(span * (nl - 1) - 128, span + 128, 0)
+
+        @pl.when((lay > 0) & (lay < nl - 1))
+        def _():
+            act(span * lay - 128, span + 256, 0)
+
+    cases(lambda *w: mask_in(*w).start())
+    cases(slopes_in)
+
+    @pl.when(lay == 0)
+    def _():
+        mki[:, 0:128] = jnp.zeros((rows, 128), jnp.int32)
+        sl[:, 0:2, 0:rows] = jnp.zeros((dirs, 2, rows, 128), F32)
+
+    @pl.when(lay == nl - 1)
+    def _():
+        mki[:, 128 * (st - 1) :] = jnp.zeros((rows, 128), jnp.int32)
+        sl[:, 2 * st - 2 :, 0:rows] = jnp.zeros((dirs, 2, rows, 128), F32)
+
+    sib[:, :, 0:8] = jnp.zeros((lays, nt, 8, 128), F32)
+    sib[:, :, rows + 25 : 40] = jnp.zeros((lays, nt, 15 - rows, 128), F32)
+    prv[:, :, HALO + 1 : 16] = jnp.zeros((lays, nt, 15 - HALO, 128), F32)
+    mb[:, HALO + 1 + two + HALO :] = jnp.zeros((nt, 56 - two - 2 * HALO - 1, 128), F32)
+
+    @pl.when(jnp.logical_not(has_prev))
+    def _():
+        prv[:, :, 0 : HALO + 1] = jnp.zeros((lays, nt, HALO + 1, 128), F32)
+        mb[:, 0 : HALO + 1] = jnp.zeros((nt, HALO + 1, 128), F32)
+        xb[0:2, :, :, 0:24] = jnp.zeros((2, lays, nt, 24, 128), F32)
+
+    @pl.when(jnp.logical_not(has_next))
+    def _():
+        nxt[...] = jnp.zeros_like(nxt)
+        mb[:, HALO + 1 + two : HALO + 1 + two + HALO] = jnp.zeros((nt, HALO, 128), F32)
+        xb[0:2, :, :, 24 + two :] = jnp.zeros((2, lays, nt, 48 - two, 128), F32)
+
+    eb[:, :, 0:8] = jnp.zeros((2, st, 8, 128), F32)
+    eb[:, :, 16:24] = jnp.zeros((2, st, 8, 128), F32)
+    q0[:, :, 0:16] = jnp.zeros((dirs, st, 16, 128), F32)
+    q0[:, :, 32:48] = jnp.zeros((dirs, st, 16, 128), F32)
     cb[:, :, :, 0:8, :] = jnp.zeros((2, lays, nt, 8, 128), F32)
 
     cases(lambda *w: mask_in(*w).wait())
@@ -178,11 +178,6 @@
     mine = HALO + 1 + rows * h
     for j in range(nt):
         mb[j, pl.ds(mine, rows), :] = ms[h, j, 0:rows, :]
-    pl.semaphore_wait(
-        barrier,
-        1 + 2 * has_prev.astype(jnp.int32) + 2 * has_next.astype(jnp.int32) + 2 * (nl - 1) + (g1 - 1) + (g2 - 1),
-    )
-
     def mask_sib():
         return rdma(
             ms.at[1 - h, :, pl.ds(0, rows)], mb.at[:, pl.ds(mine, rows)], msend.at[0], mrecv.at[0], (lay, other)
@@ -202,18 +197,6 @@
 
     sends_down = has_next & (h == 1)
     sends_up = has_prev & (h == 0)
-    mask_sib().start()
-
-    @pl.when(sends_down)
-    def _():
-        mask_down(0).start()
-        mask_down(1).start()
-
-    @pl.when(sends_up)
-    def _():
-        mask_up(0).start()
-        mask_up(1).start()
-
     cases(slopes_wait)
     first_row = rows * t
 
@@ -240,6 +223,23 @@
         return c
 
     lax.fori_loop(0, dirs, own_adjoint, 0)
+    pl.semaphore_wait(
+        barrier,
+        2 * has_prev.astype(jnp.int32) + 2 * has_next.astype(jnp.int32) + (g1 - 1) + (g2 - 1),
+    )
+
+    mask_sib().start()
+
+    @pl.when(sends_down)
+    def _():
+        mask_down(0).start()
+        mask_down(1).start()
+
+    @pl.when(sends_up)
+    def _():
+        mask_up(0).start()
+        mask_up(1).start()
+
 
     def part_sib(l):
         return rdma(
@@ -258,12 +258,13 @@
             cb.at[k, l, :, pl.ds(8, 8)], nxt.at[l], csend.at[l, 1 + k], crecv.at[l, 2], (lay, prev0 + k)
         )
 
-    def parts(l, c):
-        def block(rb, c):
+    def blocks(l, first):
+        for k8 in range(2):
+            at8 = pl.multiple_of(8 * (first + k8), 8)
             total = [[zero] * nt, [zero] * nt]
             for g in range(dirs):
                 a, s = off[l, 0, g], MARGIN + off[l, 1, g]
-                start = 8 + 8 * rb - a
+                start = 8 + at8 - a
                 turned = [pltpu.roll(q0[g, j, pl.ds(start, 8), :], s, 1) for j in range(st)]
                 keep = lane < s
                 for k in range(2):
@@ -271,25 +272,29 @@
                         total[k][j] = total[k][j] + jnp.where(keep, turned[at * k + j], turned[at * k + j + 1])
             for k in range(2):
                 for j in range(nt):
-                    cb[k, l, j, pl.ds(pl.multiple_of(8 + 8 * rb, 8), 8), :] = total[k][j]
-            return c
-
-        lax.fori_loop(0, 4, block, 0)
-        part_sib(l).start()
-
-        @pl.when(sends_down)
+                    cb[k, l, j, pl.ds(8 + at8, 8), :] = total[k][j]
+
+    def parts(step, c):
+        l, last = lax.rem(step, lays), lax.div(step, lays)
+        blocks(l, 2 * lax.rem(h + last, 2))
+
+        @pl.when((last == 0) & sends_down)
         def _():
             part_down(l, 0).start()
             part_down(l, 1).start()
 
-        @pl.when(sends_up)
+        @pl.when((last == 0) & sends_up)
         def _():
             part_up(l, 0).start()
             part_up(l, 1).start()
 
+        @pl.when(last == 1)
+        def _():
+            part_sib(l).start()
+
         return c
 
-    lax.fori_loop(0, lays, parts, 0)
+    lax.fori_loop(0, 2 * lays, parts, 0)
 
     c0 = width * (2 * lay + h)
     xcol = [c0 - MARGIN + 128 * j + lane for j in range(nt)]
@@ -304,39 +309,39 @@
         r = chip_row + start + sub
         return ((r >= 0) & (r < rows * tiles)).astype(F32)
 
-    def halo_up(x, i, l):
-        return rdma(
-            x.at[l, :, pl.ds(24, REACH)], x.at[l, :, pl.ds(24 + two, REACH)],
+    def halo_up(i, l):
+        return rdma(
+            xb.at[i, l, :, pl.ds(24, REACH)], xb.at[i, l, :, pl.ds(24 + two, REACH)],
             hsend.at[i, l, 0], hrecv.at[i, l, 0], (lay, prev0 + h),
         )
 
-    def halo_down(x, i, l):
-        return rdma(
-            x.at[l, :, pl.ds(24 + two - REACH, REACH)], x.at[l, :, pl.ds(24 - REACH, REACH)],
+    def halo_down(i, l):
+        return rdma(
+            xb.at[i, l, :, pl.ds(24 + two - REACH, REACH)], xb.at[i, l, :, pl.ds(24 - REACH, REACH)],
             hsend.at[i, l, 1], hrecv.at[i, l, 1], (lay, next0 + h),
         )
 
-    def send_halo(x, i, l):
+    def send_halo(i, l):
         @pl.when(has_prev)
         def _():
-            halo_up(x, i, l).start()
+            halo_up(i, l).start()
 
         @pl.when(has_next)
         def _():
-            halo_down(x, i, l).start()
-
-    def wait_halo(x, i, l):
+            halo_down(i, l).start()
+
+    def wait_halo(i, l):
         @pl.when(has_prev)
         def _():
-            halo_down(x, i, l).wait_recv()
+            halo_down(i, l).wait_recv()
 
         @pl.when(has_next)
         def _():
-            halo_up(x, i, l).wait_recv()
+            halo_up(i, l).wait_recv()
 
     def piece(i, l, half):
         src = ya.at[i, l, pl.ds(at * rows * half, at * rows)].reshape(rows, at, 128)
-        dst = outs[i].at[:, pl.ds(at * (2 * lay + h), at)]
+        dst = fields.at[i, :, pl.ds(at * (2 * lay + h), at)]
         return src, dst
 
     def send_pieces(i, l):
@@ -379,13 +384,13 @@
                     v = v + nxt[l, j]
                 v = v * x_in[j]
                 acc = acc + x_own[j] * (v * v)
-                x0[l, j, 24 + 8 * rb : 32 + 8 * rb, :] = v
+                xb[0, l, j, 24 + 8 * rb : 32 + 8 * rb, :] = v
                 value.append(v)
             stage(0, l, rb, value)
-        send_halo(x0, 0, l)
+        send_halo(0, l)
         return acc
 
-    bb = lax.fori_loop(0, lays, finish_b, zero)
+    sums[0] = lax.fori_loop(0, lays, finish_b, zero)
 
     mask_sib().wait_recv()
 
@@ -405,18 +410,20 @@
         right = [jnp.where(lane < 127, l[j], l[(j + 1) % n]) for j in range(n)]
         return left, right
 
-    def front(x, i):
+    def front(i):
         def smooth(l, acc):
-            wait_halo(x, i, l)
+            wait_halo(i, l)
+            for j in range(nt):
+                xw[l, j] = xb[i, l, j]
             part = zero
             for rb in range(4):
                 row = -1 + 8 * rb
-                mid = [x[l, j, 24 + row : 32 + row, :] for j in range(nt)]
+                mid = [xb[i, l, j, 24 + row : 32 + row, :] for j in range(nt)]
                 left, right = beside(mid)
                 inside = row_inside(row)
                 own = ((row + sub >= 0) & (row + sub < two)).astype(F32)
                 for j in range(nt):
-                    v = 4.0 * mid[j] - x[l, j, 23 + row : 31 + row, :] - x[l, j, 25 + row : 33 + row, :]
+                    v = 4.0 * mid[j] - xb[i, l, j, 23 + row : 31 + row, :] - xb[i, l, j, 25 + row : 33 + row, :]
                     v = (v - left[j] - right[j]) * (inside * x_in[j])
                     lb[l, j, 8 * rb : 8 * rb + 8, :] = v
                     part = part + (own * x_own[j]) * (v * v)
@@ -436,7 +443,7 @@
                 for l in range(lays):
                     a, s = off[l, 0, g], HALO - off[l, 1, g]
                     start = 15 + 8 * rb + a
-                    turned = [pltpu.roll(x[l, j, pl.ds(start, 8), :], s, 1) for j in range(nt)]
+                    turned = [pltpu.roll(xw[l, j, pl.ds(start, 8), :], s, 1) for j in range(nt)]
                     keep = lane >= s
                     total = [total[j] + jnp.where(keep, turned[j], turned[(j - 1) % nt]) for j in range(nt)]
                 inside = row_inside(8 * rb - 9)
@@ -467,7 +474,7 @@
 
         return lax.fori_loop(0, dirs, project, energy)
 
-    def back(i, x_next, first, last, acc):
+    def back(i):
         def layer(l, acc):
             for rb in range(two // 8):
                 total = [zero] * nt
@@ -484,32 +491,27 @@
                 for j in range(nt):
                     v = 4.0 * mid[j] - lb[l, j, lo - 1 : lo + 7, :] - lb[l, j, lo + 1 : lo + 9, :] - left[j] - right[j]
                     v = (total[j] + reg[l] * v) * x_in[j]
-                    if x_next is not None:
-                        acc = acc + x_own[j] * (v * v)
-                        x_next[l, j, 24 + 8 * rb : 32 + 8 * rb, :] = v
+                    acc = acc + x_own[j] * (v * v)
+                    xb[i, l, j, 24 + 8 * rb : 32 + 8 * rb, :] = v
                     value.append(v)
                 stage(i, l, rb, value)
-            if x_next is not None:
-                send_halo(x_next, 1, l)
-            else:
+
+            @pl.when(i < ITERS)
+            def _():
+                send_halo(i, l)
+
+            @pl.when(i == ITERS)
+            def _():
                 send_pieces(i, l)
+
             return acc
 
-        return lax.fori_loop(first, last, layer, acc)
-
-    e0 = front(x0, 0)
-    yy = back(1, x1, 0, lays, zero)
-    e1 = front(x1, 1)
+        return lax.fori_loop(0, lays, layer, zero)
 
     lane1 = lane[0:1]
 
     def whole(v):
         return jnp.sum(jnp.sum(v, axis=0, keepdims=True), axis=1, keepdims=True)
-
-    packed = jnp.zeros((1, 128), F32)
-    for k, v in enumerate((bb, e0, yy, e1)):
-        packed = jnp.where(lane1 == k, whole(v), packed)
-    arsrc[0:1, :] = packed
 
     def exchange(stage_id, slots, count, member):
         def one(d, c):
@@ -521,8 +523,21 @@
 
         lax.fori_loop(1, count, one, 0)
 
-    exchange(0, ar1, g1, member1)
-    back(2, None, 0, lays, zero)
+    def apply(i, c):
+        sums[1 + i] = front(i)
+
+        @pl.when(i == ITERS - 1)
+        def _():
+            packed = jnp.zeros((1, 128), F32)
+            for k, n in enumerate((0, 1, 3, 2)):
+                packed = jnp.where(lane1 == k, whole(sums[n]), packed)
+            arsrc[0:1, :] = packed
+            exchange(0, ar1, g1, member1)
+
+        sums[3 + i] = back(i + 1)
+        return c
+
+    lax.fori_loop(0, ITERS, apply, 0)
     wait_bytes(ar1, arecv.at[0])
     arsrc[8:9, :] = arsrc[0:1, :] + jnp.sum(ar1[...], axis=0, keepdims=True)
     exchange(1, ar2, g2, member2)
@@ -538,7 +553,7 @@
     k1_ref[...] = jnp.broadcast_to(a0 * a1, (1, 128))
 
     for i in range(3):
-        wait_bytes(outs[i].at[:, pl.ds(0, at * (2 * nl - 1))], trecv.at[i])
+        wait_bytes(fields.at[i, :, pl.ds(0, at * (2 * nl - 1))], trecv.at[i])
         src, dst = piece(i, 0, 0)
         pltpu.make_async_copy(src, dst, tlocal.at[i]).wait()
 
@@ -567,23 +582,31 @@
             part_up(l, 0).wait_send()
             part_up(l, 1).wait_send()
 
-        for i, x in enumerate((x0, x1)):
+        for i in range(ITERS):
 
             @pl.when(has_prev)
             def _():
-                halo_up(x, i, l).wait_send()
+                halo_up(i, l).wait_send()
 
             @pl.when(has_next)
             def _():
-                halo_down(x, i, l).wait_send()
+                halo_down(i, l).wait_send()
 
         return c
 
     lax.fori_loop(0, lays, drain, 0)
     for i in range(3):
-        wait_bytes(outs[i].at[:, pl.ds(0, at * (2 * nl - 1))], tsend.at[i])
+        wait_bytes(fields.at[i, :, pl.ds(0, at * (2 * nl - 1))], tsend.at[i])
     wait_bytes(ar1, asend.at[0])
     wait_bytes(ar2, asend.at[1])
+
+
+def combine(fields, k0, k1, est, res):
+    a, c = k0[...], k1[...]
+    for r in range(fields.shape[1]):
+        b, y1, y2 = fields[0, r], fields[1, r], fields[2, r]
+        est[r] = a * b - c * y1
+        res[r] = b - a * y1 + c * y2
 
 
 def per_device(shape, measured_slopes, valid_mask, layer_offsets, reg_weight):
@@ -597,18 +620,18 @@
     g1, g2 = nl * zs * 2, tiles // (zs * 2)
     vm = lambda *s: pltpu.VMEM(s, F32)
     dma = lambda *s: pltpu.SemaphoreType.DMA(s)
-    out = jax.ShapeDtypeStruct((rows, cols // 128, 128), F32)
+    out = jax.ShapeDtypeStruct((3, rows, cols // 128, 128), F32)
     slopes = measured_slopes.reshape(dirs, 2, rows, cols // 128, 128).transpose(0, 2, 3, 1, 4)
     slopes = slopes.reshape(dirs, rows, cols // 64, 128)
-    b, y1, y2, k0, k1 = pl.pallas_call(
+    fields, k0, k1 = pl.pallas_call(
         functools.partial(kernel, (dirs, lays, tiles, rows, cols, nl)),
-        out_shape=(out,) * 3 + (jax.ShapeDtypeStruct((1, 128), F32),) * 2,
+        out_shape=(out,) + (jax.ShapeDtypeStruct((1, 128), F32),) * 2,
         in_specs=[pl.BlockSpec(memory_space=pltpu.HBM)] * 2 + [pl.BlockSpec(memory_space=pltpu.SMEM)] * 2,
-        out_specs=(pl.BlockSpec(memory_space=pltpu.HBM),) * 3 + (pl.BlockSpec(memory_space=pltpu.VMEM),) * 2,
+        out_specs=(pl.BlockSpec(memory_space=pltpu.HBM),) + (pl.BlockSpec(memory_space=pltpu.VMEM),) * 2,
         scratch_shapes=[
             vm(dirs, 2 * st, rows + 4, 128),
             pltpu.VMEM((rows, 128 * st), jnp.int32),
-            vm(2, st, 32, 128),
+            vm(2, st, 24, 128),
             vm(dirs, st, 48, 128),
             vm(2, lays, nt, 40, 128),
             vm(lays, nt, 40, 128),
@@ -616,8 +639,9 @@
             vm(lays, nt, 8, 128),
             vm(2, nt, 16, 128),
             vm(nt, 56, 128),
+            vm(3, lays, nt, 72, 128),
             vm(lays, nt, 72, 128),
-            vm(lays, nt, 72, 128),
+            vm(5, 8, 128),
             vm(2, nt, 48, 128),
             vm(dirs, nt, 40, 128),
             vm(lays, nt, 32, 128),
@@ -632,8 +656,11 @@
             collective_id=0, has_side_effects=True, vmem_limit_bytes=56 * 1024 * 1024
         ),
     )(slopes, valid_mask, layer_offsets.transpose(1, 2, 0), reg_weight)
-    est = k0 * b - k1 * y1
-    res = b - k0 * y1 + k1 * y2
+    part = jax.ShapeDtypeStruct((rows, cols // 128, 128), F32)
+    whole = pl.BlockSpec(memory_space=pltpu.VMEM)
+    est, res = pl.pallas_call(
+        combine, out_shape=(part, part), in_specs=[whole] * 3, out_specs=(whole, whole)
+    )(fields, k0, k1)
     return est.reshape(1, rows, cols), res.reshape(1, rows, cols)
 
 

time: 51.3 us -> 50.7 us (0.988)
  other arithmetic: 1.93 us -> 0 us
  Pallas kernels: 48.5 us -> 49.8 us
    add x1 -> x0, other arithmetic: 1.93 us -> none  [per_device(): res = b - k0 * y1 + k1 * y2]
    pallas_call x0 -> x1, Pallas kernels: none -> 1.86 us  [per_device(): pl.pallas_call(combine, out_shape=(part, part), in_specs=[whole] * 3, out...]
    pallas_call x1, Pallas kernels: 48.5 us -> 48 us  [per_device(): pl.pallas_call(functools.partial(kernel, (dirs, lays, tiles, rows, cols,...]
where the time goes in v4:
time: 50.7 us; the launch traced here: 50.5 us
  Pallas kernels  49.8 us (98%)
  between operations  0.64 us (1%)
    pallas_call x1, Pallas kernels, per_device(): pl.pallas_call(functools.partial(kernel, (dirs, lays, tiles, rows, cols,...  48 us
    pallas_call x1, Pallas kernels, per_device(): pl.pallas_call(combine, out_shape=(part, part), in_specs=[whole] * 3, out...  1.86 us

profile of v4, /device:TPU:1, one launch (start us, length us, event | category | flops | bytes accessed | tf_op | source)
XLA Modules:
  0.0 50.5 jit_solution(8488148678386322661)
XLA Ops:
  0.6 48.0 %shard_map.59 = (f32[3,12,32,128]{3,2,1,0:T(8,128)}, f32[1,128]{1,0:T(1,128)}, f32[1,128]{1,0:T(1,128)}) custom-call(f32[6,12,64,128]{3,2,1,0:T(8,128)} %bitcast.8, s32[12,4096]{1,0:T(8,128)} %mask_hbm.1, s32[4,2,6]{2,1,0:T(2,128)} %bitcast.9, f32[4]{0:T(128)} %reg.1), custom_call_target="tpu_custom_call" | custom-call | tf_op jit(solution)/shard_map/pallas_call | solution.py:626
  48.6 1.9 %shard_map.60 = (f32[12,32,128]{2,1,0:T(8,128)}, f32[12,32,128]{2,1,0:T(8,128)}) custom-call(f32[3,12,32,128]{3,2,1,0:T(8,128)} %get-tuple-element.7.fields, f32[1,128]{1,0:T(1,128)} %get-tuple-element.8.k0, f32[1,128]{1,0:T(1,128)} %get-tuple-element.9.k1), custom_call_target="tpu_custom_call" | custom-call | tf_op jit(solution)/shard_map/pallas_call | solution.py:661

commit v5 on v4

--- a/solution.py
+++ b/solution.py
@@ -93,8 +93,8 @@
         greet(member2(d))
         return c
 
-    lax.fori_loop(1, g1, greet1, 0)
-    lax.fori_loop(1, g2, greet2, 0)
+    lax.fori_loop(1, g1, greet1, 0, unroll=True)
+    lax.fori_loop(1, g2, greet2, 0, unroll=True)
 
     span = 2 * width
 
@@ -521,7 +521,7 @@
             ).start()
             return c
 
-        lax.fori_loop(1, count, one, 0)
+        lax.fori_loop(1, count, one, 0, unroll=True)
 
     def apply(i, c):
         sums[1 + i] = front(i)
@@ -532,17 +532,17 @@
             for k, n in enumerate((0, 1, 3, 2)):
                 packed = jnp.where(lane1 == k, whole(sums[n]), packed)
             arsrc[0:1, :] = packed
-            exchange(0, ar1, g1, member1)
+            exchange(0, ar2, g2, member2)
 
         sums[3 + i] = back(i + 1)
         return c
 
     lax.fori_loop(0, ITERS, apply, 0)
-    wait_bytes(ar1, arecv.at[0])
-    arsrc[8:9, :] = arsrc[0:1, :] + jnp.sum(ar1[...], axis=0, keepdims=True)
-    exchange(1, ar2, g2, member2)
-    wait_bytes(ar2, arecv.at[1])
-    total = arsrc[8:9, :] + jnp.sum(ar2[...], axis=0, keepdims=True)
+    wait_bytes(ar2, arecv.at[0])
+    arsrc[8:9, :] = arsrc[0:1, :] + jnp.sum(ar2[...], axis=0, keepdims=True)
+    exchange(1, ar1, g1, member1)
+    wait_bytes(ar1, arecv.at[1])
+    total = arsrc[8:9, :] + jnp.sum(ar1[...], axis=0, keepdims=True)
     bb, e0, yy, e1 = (jnp.sum(jnp.where(lane1 == k, total, 0.0), axis=1, keepdims=True) for k in range(4))
     a0 = bb / e0
     rr = a0 * a0 * yy - bb
@@ -597,8 +597,8 @@
     lax.fori_loop(0, lays, drain, 0)
     for i in range(3):
         wait_bytes(fields.at[i, :, pl.ds(0, at * (2 * nl - 1))], tsend.at[i])
-    wait_bytes(ar1, asend.at[0])
-    wait_bytes(ar2, asend.at[1])
+    wait_bytes(ar2, asend.at[0])
+    wait_bytes(ar1, asend.at[1])
 
 
 def combine(fields, k0, k1, est, res):

time: 50.7 us -> 49.7 us (0.980)
  Pallas kernels: 49.8 us -> 48.9 us
    pallas_call x1, Pallas kernels: 48 us -> 47 us  [per_device(): pl.pallas_call(functools.partial(kernel, (dirs, lays, tiles, rows, cols,...]
where the time goes in v5:
time: 49.7 us; the launch traced here: 49.5 us
  Pallas kernels  48.9 us (98%)
  between operations  0.64 us (1%)
    pallas_call x1, Pallas kernels, per_device(): pl.pallas_call(functools.partial(kernel, (dirs, lays, tiles, rows, cols,...  47 us
    pallas_call x1, Pallas kernels, per_device(): pl.pallas_call(combine, out_shape=(part, part), in_specs=[whole] * 3, out...  1.86 us

profile of v5, /device:TPU:1, one launch (start us, length us, event | category | flops | bytes accessed | tf_op | source)
XLA Modules:
  0.0 49.5 jit_solution(7654949488481971596)
XLA Ops:
  0.6 47.0 %shard_map.59 = (f32[3,12,32,128]{3,2,1,0:T(8,128)}, f32[1,128]{1,0:T(1,128)}, f32[1,128]{1,0:T(1,128)}) custom-call(f32[6,12,64,128]{3,2,1,0:T(8,128)} %bitcast.8, s32[12,4096]{1,0:T(8,128)} %mask_hbm.1, s32[4,2,6]{2,1,0:T(2,128)} %bitcast.9, f32[4]{0:T(128)} %reg.1), custom_call_target="tpu_custom_call" | custom-call | tf_op jit(solution)/shard_map/pallas_call | solution.py:626
  47.6 1.9 %shard_map.60 = (f32[12,32,128]{2,1,0:T(8,128)}, f32[12,32,128]{2,1,0:T(8,128)}) custom-call(f32[3,12,32,128]{3,2,1,0:T(8,128)} %get-tuple-element.7.fields, f32[1,128]{1,0:T(1,128)} %get-tuple-element.8.k0, f32[1,128]{1,0:T(1,128)} %get-tuple-element.9.k1), custom_call_target="tpu_custom_call" | custom-call | tf_op jit(solution)/shard_map/pallas_call | solution.py:661

commit v6 on v5

--- a/solution.py
+++ b/solution.py
@@ -413,6 +413,11 @@
     def front(i):
         def smooth(l, acc):
             wait_halo(i, l)
+
+            @pl.when(l >= lays // 2)
+            def _():
+                send_pieces(i, l - lays // 2)
+
             for j in range(nt):
                 xw[l, j] = xb[i, l, j]
             part = zero
@@ -435,7 +440,7 @@
             send_pieces(i, l)
             return c
 
-        lax.fori_loop(0, lays, give, 0)
+        lax.fori_loop(lays // 2, lays, give, 0)
 
         def project(g, acc):
             for rb in range(6):
@@ -541,6 +546,54 @@
     wait_bytes(ar2, arecv.at[0])
     arsrc[8:9, :] = arsrc[0:1, :] + jnp.sum(ar2[...], axis=0, keepdims=True)
     exchange(1, ar1, g1, member1)
+    mask_sib().wait_send()
+
+    @pl.when(sends_down)
+    def _():
+        mask_down(0).wait_send()
+        mask_down(1).wait_send()
+
+    @pl.when(sends_up)
+    def _():
+        mask_up(0).wait_send()
+        mask_up(1).wait_send()
+
+    def drain(l, c):
+        part_sib(l).wait_send()
+
+        @pl.when(sends_down)
+        def _():
+            part_down(l, 0).wait_send()
+            part_down(l, 1).wait_send()
+
+        @pl.when(sends_up)
+        def _():
+            part_up(l, 0).wait_send()
+            part_up(l, 1).wait_send()
+
+        for i in range(ITERS):
+
+            @pl.when(has_prev)
+            def _():
+                halo_up(i, l).wait_send()
+
+            @pl.when(has_next)
+            def _():
+                halo_down(i, l).wait_send()
+
+        return c
+
+    lax.fori_loop(0, lays, drain, 0)
+
+    def landed(i):
+        wait_bytes(fields.at[i, :, pl.ds(0, at * (2 * nl - 1))], trecv.at[i])
+        src, dst = piece(i, 0, 0)
+        pltpu.make_async_copy(src, dst, tlocal.at[i]).wait()
+        wait_bytes(fields.at[i, :, pl.ds(0, at * (2 * nl - 1))], tsend.at[i])
+
+    landed(0)
+    landed(1)
+    wait_bytes(ar2, asend.at[0])
     wait_bytes(ar1, arecv.at[1])
     total = arsrc[8:9, :] + jnp.sum(ar1[...], axis=0, keepdims=True)
     bb, e0, yy, e1 = (jnp.sum(jnp.where(lane1 == k, total, 0.0), axis=1, keepdims=True) for k in range(4))
@@ -552,52 +605,7 @@
     k0_ref[...] = jnp.broadcast_to(a0 + a1 * grown, (1, 128))
     k1_ref[...] = jnp.broadcast_to(a0 * a1, (1, 128))
 
-    for i in range(3):
-        wait_bytes(fields.at[i, :, pl.ds(0, at * (2 * nl - 1))], trecv.at[i])
-        src, dst = piece(i, 0, 0)
-        pltpu.make_async_copy(src, dst, tlocal.at[i]).wait()
-
-    mask_sib().wait_send()
-
-    @pl.when(sends_down)
-    def _():
-        mask_down(0).wait_send()
-        mask_down(1).wait_send()
-
-    @pl.when(sends_up)
-    def _():
-        mask_up(0).wait_send()
-        mask_up(1).wait_send()
-
-    def drain(l, c):
-        part_sib(l).wait_send()
-
-        @pl.when(sends_down)
-        def _():
-            part_down(l, 0).wait_send()
-            part_down(l, 1).wait_send()
-
-        @pl.when(sends_up)
-        def _():
-            part_up(l, 0).wait_send()
-            part_up(l, 1).wait_send()
-
-        for i in range(ITERS):
-
-            @pl.when(has_prev)
-            def _():
-                halo_up(i, l).wait_send()
-
-            @pl.when(has_next)
-            def _():
-                halo_down(i, l).wait_send()
-
-        return c
-
-    lax.fori_loop(0, lays, drain, 0)
-    for i in range(3):
-        wait_bytes(fields.at[i, :, pl.ds(0, at * (2 * nl - 1))], tsend.at[i])
-    wait_bytes(ar2, asend.at[0])
+    landed(2)
     wait_bytes(ar1, asend.at[1])
 
 

time: 49.7 us -> 49.2 us (0.990)
  Pallas kernels: 48.9 us -> 48.4 us
where the time goes in v6:
time: 49.2 us; the launch traced here: 49 us
  Pallas kernels  48.4 us (98%)
  between operations  0.64 us (1%)
    pallas_call x1, Pallas kernels, per_device(): pl.pallas_call(functools.partial(kernel, (dirs, lays, tiles, rows, cols,...  46.5 us
    pallas_call x1, Pallas kernels, per_device(): pl.pallas_call(combine, out_shape=(part, part), in_specs=[whole] * 3, out...  1.86 us

profile of v6, /device:TPU:1, one launch (start us, length us, event | category | flops | bytes accessed | tf_op | source)
XLA Modules:
  0.0 49.0 jit_solution(5110770702245670901)
XLA Ops:
  0.6 46.5 %shard_map.59 = (f32[3,12,32,128]{3,2,1,0:T(8,128)}, f32[1,128]{1,0:T(1,128)}, f32[1,128]{1,0:T(1,128)}) custom-call(f32[6,12,64,128]{3,2,1,0:T(8,128)} %bitcast.8, s32[12,4096]{1,0:T(8,128)} %mask_hbm.1, s32[4,2,6]{2,1,0:T(2,128)} %bitcast.9, f32[4]{0:T(128)} %reg.1), custom_call_target="tpu_custom_call" | custom-call | tf_op jit(solution)/shard_map/pallas_call | solution.py:634
  47.1 1.9 %shard_map.60 = (f32[12,32,128]{2,1,0:T(8,128)}, f32[12,32,128]{2,1,0:T(8,128)}) custom-call(f32[3,12,32,128]{3,2,1,0:T(8,128)} %get-tuple-element.7.fields, f32[1,128]{1,0:T(1,128)} %get-tuple-element.8.k0, f32[1,128]{1,0:T(1,128)} %get-tuple-element.9.k1), custom_call_target="tpu_custom_call" | custom-call | tf_op jit(solution)/shard_map/pallas_call | solution.py:669

commit v7 on v6

--- a/solution.py
+++ b/solution.py
@@ -144,7 +144,7 @@
     sib[:, :, 0:8] = jnp.zeros((lays, nt, 8, 128), F32)
     sib[:, :, rows + 25 : 40] = jnp.zeros((lays, nt, 15 - rows, 128), F32)
     prv[:, :, HALO + 1 : 16] = jnp.zeros((lays, nt, 15 - HALO, 128), F32)
-    mb[:, HALO + 1 + two + HALO :] = jnp.zeros((nt, 56 - two - 2 * HALO - 1, 128), F32)
+    mb[:, HALO + 1 + two + HALO : 56] = jnp.zeros((nt, 56 - two - 2 * HALO - 1, 128), F32)
 
     @pl.when(jnp.logical_not(has_prev))
     def _():
@@ -642,11 +642,11 @@
             vm(2, st, 24, 128),
             vm(dirs, st, 48, 128),
             vm(2, lays, nt, 40, 128),
-            vm(lays, nt, 40, 128),
-            vm(lays, nt, 16, 128),
+            vm(lays, nt, 48, 128),
+            vm(lays, nt, 24, 128),
             vm(lays, nt, 8, 128),
             vm(2, nt, 16, 128),
-            vm(nt, 56, 128),
+            vm(nt, 64, 128),
             vm(3, lays, nt, 72, 128),
             vm(lays, nt, 72, 128),
             vm(5, 8, 128),

time: 49.2 us -> 49.2 us (level)
  no operation moved by 1% of the time
where the time goes in v7:
time: 49.2 us; the launch traced here: 49 us
  Pallas kernels  48.4 us (98%)
  between operations  0.64 us (1%)
    pallas_call x1, Pallas kernels, per_device(): pl.pallas_call(functools.partial(kernel, (dirs, lays, tiles, rows, cols,...  46.5 us
    pallas_call x1, Pallas kernels, per_device(): pl.pallas_call(combine, out_shape=(part, part), in_specs=[whole] * 3, out...  1.86 us

profile of v7, /device:TPU:1, one launch (start us, length us, event | category | flops | bytes accessed | tf_op | source)
XLA Modules:
  0.0 49.0 jit_solution(8834111044968626078)
XLA Ops:
  0.6 46.5 %shard_map.59 = (f32[3,12,32,128]{3,2,1,0:T(8,128)}, f32[1,128]{1,0:T(1,128)}, f32[1,128]{1,0:T(1,128)}) custom-call(f32[6,12,64,128]{3,2,1,0:T(8,128)} %bitcast.8, s32[12,4096]{1,0:T(8,128)} %mask_hbm.1, s32[4,2,6]{2,1,0:T(2,128)} %bitcast.9, f32[4]{0:T(128)} %reg.1), custom_call_target="tpu_custom_call" | custom-call | tf_op jit(solution)/shard_map/pallas_call | solution.py:634
  47.2 1.9 %shard_map.60 = (f32[12,32,128]{2,1,0:T(8,128)}, f32[12,32,128]{2,1,0:T(8,128)}) custom-call(f32[3,12,32,128]{3,2,1,0:T(8,128)} %get-tuple-element.7.fields, f32[1,128]{1,0:T(1,128)} %get-tuple-element.8.k0, f32[1,128]{1,0:T(1,128)} %get-tuple-element.9.k1), custom_call_target="tpu_custom_call" | custom-call | tf_op jit(solution)/shard_map/pallas_call | solution.py:669
